TPU v7x, 32 devices: a whole 2x2x4 slice. The times are simulated.
32 devices in a mesh: section: 4 (over z), fsdp: 8 (over y, x, core).
Axes of the slice: x: 2, y: 2, z: 4, core: 2. Of those that a mesh axis runs over, the one named last changes fastest.
Arguments:
- feats: bfloat16 [4, 8, 256, 1536], P(None, 'fsdp'), may hold values from -6 to 6
- w_in: bfloat16 [2, 4, 1536, 3072], P(None, 'section', 'fsdp'), may hold values from -0.15625 to 0.15625
- dw_kernel: bfloat16 [2, 4, 31, 1536], P(None, 'section', None, 'fsdp'), may hold values from -1 to 1
- mask_embed: bfloat16 [1536], replicated, may hold values from -6 to 6
- w_ctx: bfloat16 [1536, 768], replicated, may hold values from -0.15625 to 0.15625
- w_tgt: bfloat16 [1536, 768], replicated, may hold values from -0.15625 to 0.15625
- mask_starts: int32 [4, 8, 12], P(None, 'fsdp'), may hold values from 0 to 246
- distractors: int32 [4, 8, 256, 100], P(None, 'fsdp', 'section'), may hold values from 0 to 255
Outputs:
- frame_loss: float32 [4, 8, 256], P(None, 'fsdp', 'section')
All inputs are finite; a program needn't handle non-finite values.
Results may differ from a plain program's by a relative error of at most 0.0054.
Values may be sent and summed in bfloat16 or wider, within the bound.
No kernel may reach another device: no remote copies, remote signals or barrier semaphores. Data moves between devices by JAX's collectives and lax.ppermute only.
A program may use at most 128 MiB of HBM per device.

v0:
```python
import functools

import jax
import jax.numpy as jnp
import ml_dtypes
import numpy as np
from jax import lax
from jax.experimental import pallas as pl
from jax.experimental.pallas import tpu as pltpu
from jax.sharding import PartitionSpec as P

MASK_LEN = 10
LANES = 128
PAD = 16
VMEM_LIMIT = 20 * 1024 * 1024
LATE_VMEM_LIMIT = 48 * 1024 * 1024


BLOCK = 128
WINDOW = BLOCK + 2 * PAD
HALF = WINDOW // 2


def transforms(taps):
    freq = np.arange(HALF)[:, None] * (2 * np.pi / WINDOW)
    spot = np.arange(WINDOW)[None, :]
    forward = np.concatenate([np.cos(freq * spot), -np.sin(freq * spot)])
    forward[HALF] = (-1.0) ** np.arange(WINDOW)
    inverse = forward[:, :BLOCK].T
    at = np.arange(taps)[None, :] + PAD - taps // 2
    scale = np.full((HALF, 1), 2.0 / WINDOW)
    scale[0] = 1.0 / WINDOW
    real, imag = np.cos(freq * at) * scale, np.sin(freq * at) * scale
    last = real.copy()
    last[0] = (-1.0) ** at[0] / WINDOW
    return forward, inverse, np.concatenate([real, imag, last])


def sigmoid(v):
    return 0.5 + 0.5 * jnp.tanh(0.5 * v)


def layer_body(entry, kinds, fresh_slot, recvs, spare, base, flags, *refs):
    refs = list(refs)
    fresh = refs.pop(0) if fresh_slot is not None else None
    recv = [refs.pop(0) for _ in range(recvs)]
    sources = [[refs.pop(0) for _ in range(count)] for _, _, count in kinds]
    starts = refs.pop(0)
    k_refs = [refs.pop(0) for _ in kinds]
    forward, inverse = refs.pop(0), refs.pop(0)
    del refs[:spare]
    out_ref, mark_ref, normed, wbuf, glu, w_sem = (refs.pop(0) for _ in range(6))
    x_ref, x_sem = refs if refs else (recv[0], None)
    chunks, width, part = wbuf.shape
    part = part // 2
    frames = x_ref.shape[0]
    valid = flags[entry, 0]
    turn = flags[entry, 1]

    def weight_copies(kind, source, j, side):
        target, sem = wbuf.at[j, :, pl.ds(side * part, part)], w_sem.at[j]
        cols = pl.ds(pl.multiple_of(side * width + j * part, part), part)
        if kind == "rows":
            return [pltpu.make_async_copy(source[0].at[:, cols], target, sem)]
        copies = []
        for i, piece in enumerate(source):
            size = piece.shape[0]
            place = pl.ds(pl.multiple_of(starts[i], size), size)
            into = wbuf.at[j, place, pl.ds(side * part, part)]
            copies.append(pltpu.make_async_copy(piece.at[:, cols], into, sem))
        return copies

    def start_weights(j):
        def issue(kind, source):
            for side in range(2):
                for copy in weight_copies(kind, source, j, side):
                    copy.start()

        for (which, kind, _), source in zip(kinds, sources):
            if len(kinds) == 1:
                issue(kind, source)
            else:
                pl.when(turn == which)(functools.partial(issue, kind, source))

    def wait_weights(j):
        pltpu.make_async_copy(wbuf.at[j], wbuf.at[j], w_sem.at[j]).wait()

    def project(j, slot):
        both = jnp.dot(normed[...], wbuf[j], preferred_element_type=jnp.float32)
        gated = both[:, :part] * sigmoid(both[:, part:])
        glu[slot, PAD : PAD + frames, :] = gated.astype(jnp.bfloat16)

    def taps(i, cols):
        rows = slice(HALF * i, HALF * (i + 1))
        chosen = k_refs[0][rows, cols]
        for (which, _, _), k_ref in zip(kinds[1:], k_refs[1:]):
            chosen = jnp.where(turn == which, k_ref[rows, cols], chosen)
        return chosen

    def mix(j, slot):
        cols = pl.ds(pl.multiple_of(j * part, part), part)
        real, imag, last = (taps(i, cols) for i in range(3))
        for row in range(0, frames, BLOCK):
            window = glu[slot, row : row + WINDOW, :]
            freq = jnp.dot(forward[...], window, preferred_element_type=jnp.float32)
            up, low = freq[:HALF], freq[HALF:]
            freq = jnp.concatenate([up * real - low * imag, up * imag + low * last], axis=0)
            conv = jnp.dot(
                inverse[...], freq.astype(jnp.bfloat16), preferred_element_type=jnp.float32
            )
            base = x_ref[row : row + BLOCK, cols].astype(jnp.float32)
            out_ref[row : row + BLOCK, cols] = (base + conv * sigmoid(conv)).astype(jnp.bfloat16)

    @pl.when(valid == 1)
    def _():
        ahead = min(3, chunks)
        if x_sem is not None:
            options = ([] if fresh is None else [fresh]) + recv
            first = base
            for i, option in enumerate(options):

                @pl.when(flags[entry, 2] == first + i)
                def _(option=option):
                    pltpu.make_async_copy(option, x_ref, x_sem).start()

        for j in range(ahead):
            start_weights(j)
        zeros = jnp.zeros((2, PAD, part), jnp.bfloat16)
        glu[:, 0:PAD, :] = zeros
        glu[:, PAD + frames :, :] = zeros
        if x_sem is not None:
            pltpu.make_async_copy(x_ref, x_ref, x_sem).wait()
        for row in range(0, frames, 64):
            values = x_ref[row : row + 64, :].astype(jnp.float32)
            center = jnp.mean(values, axis=1, keepdims=True)
            moved = values - center
            spread = jnp.mean(moved * moved, axis=1, keepdims=True)
            normed[row : row + 64, :] = (moved * lax.rsqrt(spread + 1e-05)).astype(jnp.bfloat16)
        wait_weights(0)
        project(0, 0)

        @pl.loop(0, chunks - 1)
        def _(j):
            wait_weights(j + 1)

            @pl.when(j + ahead < chunks)
            def _():
                start_weights(j + ahead)

            mix(j, j % 2)
            project(j + 1, (j + 1) % 2)

        mix(chunks - 1, (chunks - 1) % 2)

    mark_ref[...] = jnp.zeros(mark_ref.shape, mark_ref.dtype)


def layer(
    entry, flags, fresh, fresh_slot, recvs, weights, starts, kernels, matrices, spare=(), base=0,
    outside=False, limit=VMEM_LIMIT,
):
    frames, width = recvs[0].shape if recvs else fresh.shape
    part = 256
    chunks = width // part
    anywhere = pl.BlockSpec(memory_space=pl.ANY)
    local = pl.BlockSpec(memory_space=pltpu.VMEM)
    smem = pl.BlockSpec(memory_space=pltpu.SMEM)
    far = pl.BlockSpec(memory_space=pltpu.HBM)
    select = fresh_slot is not None or len(recvs) > 1 or outside
    operands, specs = [flags], [smem]
    if fresh_slot is not None:
        operands.append(fresh)
        specs.append(far)
    operands += recvs
    specs += [far if outside else anywhere if select else local] * len(recvs)
    for _, kind, arrays in weights:
        operands += arrays
        specs += [far if kind == "rows" else anywhere] * len(arrays)
    operands += [starts, *kernels, *matrices, *spare]
    specs += [smem] + [local] * (len(kernels) + len(matrices)) + [anywhere] * len(spare)
    scratch = [
        pltpu.VMEM((frames, width), jnp.bfloat16),
        pltpu.VMEM((chunks, width, 2 * part), jnp.bfloat16),
        pltpu.VMEM((2, frames + 2 * PAD, part), jnp.bfloat16),
        pltpu.SemaphoreType.DMA((chunks,)),
    ]
    if select:
        scratch += [pltpu.VMEM((frames, width), jnp.bfloat16), pltpu.SemaphoreType.DMA]
    kinds = [(turn, kind, len(arrays)) for turn, kind, arrays in weights]
    return pl.pallas_call(
        functools.partial(
            layer_body, entry, kinds, fresh_slot, len(recvs), len(spare), base
        ),
        in_specs=specs,
        out_specs=[local, local],
        out_shape=[
            jax.ShapeDtypeStruct((frames, width), jnp.bfloat16),
            jax.ShapeDtypeStruct((8, LANES), jnp.float32),
        ],
        scratch_shapes=scratch,
        compiler_params=pltpu.CompilerParams(vmem_limit_bytes=limit),
        cost_estimate=pl.CostEstimate(
            flops=4 * frames * width * width, bytes_accessed=4 * width * width, transcendentals=0
        ),
        name="layer",
    )(*operands)


def transform_body(m_ref, k_ref, out_ref):
    total = jnp.dot(m_ref[0], k_ref[...], preferred_element_type=jnp.float32)
    for part in range(1, m_ref.shape[0]):
        total = total + jnp.dot(m_ref[part], k_ref[...], preferred_element_type=jnp.float32)
    out_ref[...] = total


def transformed(matrix, kernel):
    return pl.pallas_call(
        transform_body,
        out_shape=jax.ShapeDtypeStruct((matrix.shape[1], kernel.shape[1]), jnp.float32),
        compiler_params=pltpu.CompilerParams(vmem_limit_bytes=VMEM_LIMIT),
        name="transformed",
    )(matrix, kernel)


def unit_rows(values):
    return (values * lax.rsqrt(jnp.sum(values * values, axis=-1, keepdims=True) + 1e-06)).astype(
        jnp.bfloat16
    )


def target_body(wanted, flags, feats, w_tgt, *refs):
    out, feats_ref, w_ref, out_ref, sems = refs[-5:]

    @pl.when(flags[0, 4] == wanted)
    def _():
        load_w = pltpu.make_async_copy(w_tgt, w_ref, sems.at[0])
        load_x = pltpu.make_async_copy(feats, feats_ref, sems.at[1])
        load_w.start()
        load_x.start()
        load_w.wait()
        load_x.wait()

        @pl.loop(0, feats_ref.shape[0])
        def _(slot):
            out_ref[slot] = unit_rows(
                jnp.dot(feats_ref[slot], w_ref[...], preferred_element_type=jnp.float32)
            )

        back = pltpu.make_async_copy(out_ref, out, sems.at[2])
        back.start()
        back.wait()


def targets(flags, feats, w_tgt, wanted, spare, earlier=None):
    operands = [flags, feats, w_tgt, spare] + ([] if earlier is None else [earlier])
    anywhere = pl.BlockSpec(memory_space=pl.ANY)
    shape = feats.shape[:2] + w_tgt.shape[1:]
    return pl.pallas_call(
        functools.partial(target_body, wanted),
        in_specs=[pl.BlockSpec(memory_space=pltpu.SMEM)] + [anywhere] * (len(operands) - 1),
        out_specs=anywhere,
        out_shape=jax.ShapeDtypeStruct(shape, jnp.bfloat16),
        scratch_shapes=[
            pltpu.VMEM(feats.shape, jnp.bfloat16),
            pltpu.VMEM(w_tgt.shape, jnp.bfloat16),
            pltpu.VMEM(shape, jnp.bfloat16),
            pltpu.SemaphoreType.DMA((3,)),
        ],
        input_output_aliases={} if earlier is None else {4: 0},
        compiler_params=pltpu.CompilerParams(vmem_limit_bytes=VMEM_LIMIT),
        cost_estimate=pl.CostEstimate(
            flops=2 * feats.size * w_tgt.shape[1],
            bytes_accessed=2 * (feats.size + w_tgt.size),
            transcendentals=0,
        ),
        name="targets",
    )(*operands)


def loss_body(slot, count, flags, x_ref, w_ref, tgt_ref, pick_ref, out_ref):
    frames = x_ref.shape[0]

    @pl.when(flags[0, 3] == 1)
    def _():
        ctx = unit_rows(jnp.dot(x_ref[...], w_ref[...], preferred_element_type=jnp.float32))
        sims = lax.dot_general(
            ctx, tgt_ref[slot], (((1,), (1,)), ((), ())), preferred_element_type=jnp.float32
        )
        row = lax.broadcasted_iota(jnp.int32, sims.shape, 0)
        col = lax.broadcasted_iota(jnp.int32, sims.shape, 1)
        positive = jnp.sum(jnp.where(row == col, sims, 0.0), axis=1, keepdims=True) * 10.0
        picks = pick_ref[slot]
        lane = picks % LANES
        block = picks // LANES
        negative = jnp.zeros(picks.shape, jnp.float32)
        for part in range(frames // LANES):
            found = jnp.take_along_axis(sims[:, part * LANES : (part + 1) * LANES], lane, axis=1)
            negative = jnp.where(block == part, found, negative)
        place = lax.broadcasted_iota(jnp.int32, picks.shape, 1)
        terms = jnp.where(place < count, jnp.exp(negative * 10.0), 0.0)
        total = jnp.exp(positive) + jnp.sum(terms, axis=1, keepdims=True)
        wide = jnp.broadcast_to(jnp.log(total) - positive, (frames, LANES))
        out_ref[...] = wide.T[0:1, :]


def loss_rows(slot, flags, x, w_ctx, tgt, picks, count):
    frames = x.shape[0]
    whole = pl.BlockSpec(memory_space=pltpu.VMEM)
    return pl.pallas_call(
        functools.partial(loss_body, slot, count),
        in_specs=[pl.BlockSpec(memory_space=pltpu.SMEM)] + [whole] * 4,
        out_specs=whole,
        out_shape=jax.ShapeDtypeStruct((1, frames), jnp.float32),
        compiler_params=pltpu.CompilerParams(vmem_limit_bytes=VMEM_LIMIT),
        name="loss",
    )(flags, x, w_ctx, tgt, picks)


def swap(block, axis, mask):
    return lax.ppermute(block, axis, [(i, i ^ mask) for i in range(lax.axis_size(axis))])


def chip_pieces(block, axis):
    size = lax.axis_size(axis)
    other = swap(block, axis, 1)
    odd = lax.axis_index(axis) % 2 == 1
    both = jnp.concatenate([jnp.where(odd, other, block), jnp.where(odd, block, other)], axis=0)
    return [swap(both, axis, mask) if mask else both for mask in range(0, size, 2)]


def in_order(pieces, axis):
    chip = lax.axis_index(axis) // 2
    mask = 1
    while mask < len(pieces):
        upper = chip // mask % 2 == 1
        pieces = [jnp.where(upper, pieces[i ^ mask], pieces[i]) for i in range(len(pieces))]
        mask *= 2
    return jnp.concatenate(pieces, axis=0)


def crossed(block, axis, small, prepare):
    size = lax.axis_size(axis)
    me = lax.axis_index(axis)
    odd = me % 2
    ahead = [(i, i ^ (2 if i % 2 else 4)) for i in range(size)]
    other = [(i, i ^ (4 if i % 2 else 2)) for i in range(size)]
    near = lax.ppermute(block, axis, ahead)
    block, near, small = lax.optimization_barrier((block, near, small))
    far = lax.ppermute(near, axis, other)
    side = lax.ppermute(block, axis, other)
    small = prepare(small)
    first, second = 4 - 2 * odd, 2 + 2 * odd
    pieces = [block, near, side, far]
    masks = [0, first, second, 6]
    pieces += [swap(piece, axis, 1) for piece in pieces]
    masks += [1, second ^ 1, first ^ 1, 7]
    starts = jnp.stack([(me ^ mask) * block.shape[0] for mask in masks]).astype(jnp.int32)
    return pieces, starts, small


def on_device(feats, w_in, dw_kernel, mask_embed, w_ctx, w_tgt, mask_starts, distractors):
    sections = lax.axis_size("section")
    section = lax.axis_index("section")
    size = lax.axis_size("fsdp")
    micro = feats.shape[0]
    frames = feats.shape[2]
    repeats = w_in.shape[0]
    last = sections - 1
    feats_local = feats[:, 0]


    def work(step, s):
        offset = step - s
        if offset < 0:
            return None
        turn, slot = offset // sections, offset % sections
        return (turn, slot) if slot < micro and turn < repeats else None

    steps = repeats * sections + micro - 1
    plans = [[work(step, s) for s in range(sections)] for step in range(steps)]
    table = [
        [
            [
                int(plan[s] is not None),
                0 if plan[s] is None else plan[s][0],
                int(not (s == 0 and plan[s] is not None and plan[s][0] == 0)),
                int(s == last),
                0,
            ]
            for plan in plans + plans[:1]
        ]
        for s in range(sections)
    ]
    odd = lax.axis_index("fsdp") % 2
    flags = lax.dynamic_index_in_dim(jnp.array(table, jnp.int32), section, 0, keepdims=False)
    lanes = lax.broadcasted_iota(jnp.int32, flags.shape, 1)
    entries = lax.broadcasted_iota(jnp.int32, flags.shape, 0)
    off = (lanes == 0) & (((entries == 0) & (odd == 1)) | ((entries == steps) & (odd == 0)))
    flags = jnp.where(lanes == 4, odd, jnp.where(off, 0, flags))
    middle = micro + 1
    split = (entries == 1) | (entries == middle + 1)
    flags = jnp.where(split & (lanes == 2) & (flags == 1), 1 + odd, flags)

    spots = jnp.arange(frames, dtype=jnp.int32)
    begins = mask_starts[:, 0][:, :, None]
    covered = jnp.any(
        (spots[None, None, :] >= begins) & (spots[None, None, :] < begins + MASK_LEN), axis=1
    )
    masked_in = [
        jnp.where(covered[slot][:, None], mask_embed[None, :], feats_local[slot])
        for slot in range(micro)
    ]

    taps = dw_kernel.shape[2]
    own = jnp.pad(dw_kernel[:, 0], ((0, 0), (0, -taps % 8), (0, 0)))
    own = jnp.transpose(own, (2, 0, 1))
    ring = chip_pieces(own.reshape(own.shape[0], -1), "fsdp")
    forward, inverse, rest = transforms(taps)
    rest = np.pad(rest, ((0, 0), (0, -taps % 8)))
    of_taps = []
    for _ in range(3):
        of_taps.append(rest.astype(ml_dtypes.bfloat16))
        rest = rest - of_taps[-1].astype(np.float64)
    of_taps = jnp.asarray(np.stack(of_taps))
    mats = (jnp.asarray(forward, jnp.bfloat16), jnp.asarray(inverse, jnp.bfloat16))

    def prepare(small):
        ring, w_late = small
        full_k = in_order(ring, "fsdp").reshape(feats.shape[3], repeats, -1)
        full_k = jnp.transpose(full_k, (1, 2, 0))
        kernels = [transformed(of_taps, full_k[0])] + [full_k[turn] for turn in range(1, repeats)]
        later = [w_late[turn, 0] for turn in range(1, repeats)]
        return kernels, masked_in, flags, mats, later

    small = (ring, w_in)
    if size == 8:
        pieces, starts, small = crossed(w_in[0, 0], "fsdp", small, prepare)
        kind = "pieces"
    else:
        pieces = [lax.all_gather(w_in[0, 0], "fsdp", axis=0, tiled=True)]
        starts = jnp.zeros((1,), jnp.int32)
        kind = "rows"
        small = prepare(small)
    pieces, (starts, small) = lax.optimization_barrier((pieces, (starts, small)))
    kernels, masked_in, flags, mats, later = small

    def hop_of(block, route, parity):
        route = [(a * size + f, b * size + f) for a, b in route for f in range(parity, size, 2)]
        return lax.ppermute(block, ("section", "fsdp"), route)

    weights = [(0, kind, pieces)]
    for turn in range(1, repeats):
        rows = lax.all_gather(later[turn - 1], "fsdp", axis=0, tiled=True)
        weights.append((turn, "rows", [rows]))

    early, mark = layer(
        0, flags, masked_in[0], 0, [], weights[:1], starts, kernels[:1], mats
    )
    token = lax.ppermute(mark, "fsdp", [(i, i + 1) for i in range(0, size, 2)])
    early = hop_of(early, [(0, 1)], 0)
    tgt = targets(flags, feats_local, w_tgt, 1, token)
    result, mark = layer(
        steps, flags, masked_in[0], 0, [], weights[:1], starts, kernels[:1], mats, (tgt,)
    )
    state = [early, hop_of(result, [(0, 1)], 1)]
    count = distractors.shape[3]
    parts = []

    losses = []
    for step, plan in enumerate(plans):
        if step == 0:
            continue
        turns = sorted({item[0] for item in plan if item is not None})
        slot = plan[0][1] if plan[0] is not None and plan[0][0] == 0 else None
        used = [weights[turn] for turn in turns]
        k_used = [kernels[turn] for turn in turns]
        spare = ()
        if 1 < step <= last + 1:
            picks, mark = lax.optimization_barrier((distractors[:, 0], mark))
            parts.append(lax.ppermute(picks, "section", [(step - 2, last)]))
            spare = (mark, parts[-1])
        if step == 2:
            tgt = targets(flags, feats_local, w_tgt, 0, mark, tgt)
            spare += (tgt,)
        if step == micro:
            rows = [arrays for _, _, arrays in weights[1:]]
            kernels[1:], rows = lax.optimization_barrier((kernels[1:], rows))
            kernels[1:] = [transformed(of_taps, kernel) for kernel in kernels[1:]]
            weights[1:] = [(turn + 1, "rows", arrays) for turn, arrays in enumerate(rows)]
            used = [weights[turn] for turn in turns]
            k_used = [kernels[turn] for turn in turns]
        base = int(step == micro)
        if step == middle + 1:
            spare, base = (token,), 1
        result, mark = layer(
            step, flags, None if slot is None else masked_in[slot], slot, state, used, starts, k_used, mats, spare, base, step == micro,
            VMEM_LIMIT if step < micro else LATE_VMEM_LIMIT,
        )
        if step == last + 1:
            picks = jnp.concatenate(parts + [distractors[:, 0]], axis=1)
            picks = jnp.pad(picks, ((0, 0), (0, 0), (0, -count % LANES)))
        ends = plan[last]
        if ends is not None and ends[0] == repeats - 1:
            losses.append(loss_rows(ends[1], flags, result, w_ctx, tgt, picks, count))
        state = []
        route = []
        for s, item in enumerate(plan):
            if item is not None and not (s == last and item[0] == repeats - 1):
                route.append((s, (s + 1) % sections))
        if route and step == middle:
            state = [hop_of(result, route, 0)]
            token = lax.ppermute(
                state[0][:16, :LANES], "fsdp", [(i, i + 1) for i in range(0, size, 2)]
            )
            result, token = lax.optimization_barrier((result, token))
            state.append(hop_of(result, route, 1))
        elif route:
            state = [lax.ppermute(result, "section", route)]

    loss = jnp.concatenate(losses, axis=0)
    share = frames // sections
    mine = jnp.zeros((micro, share), jnp.float32)
    for s in range(sections):
        cut = loss[:, s * share : (s + 1) * share]
        if s == last:
            mine = mine + jnp.where(section == last, cut, 0.0)
        else:
            mine = mine + lax.ppermute(cut, "section", [(last, s)])
    return mine[:, None, :]


def solution(mesh):
    placed = (
        P(None, "fsdp", None, None),
        P(None, "section", "fsdp", None),
        P(None, "section", None, "fsdp"),
        P(),
        P(),
        P(),
        P(None, "fsdp", None),
        P(None, "fsdp", "section", None),
    )
    return jax.shard_map(
        on_device, mesh=mesh, in_specs=placed, out_specs=P(None, "fsdp", "section"), check_vma=False
    )
```

profile of v0, /device:TPU:1, one launch (start us, length us, event | category | flops | bytes accessed | tf_op | source)
XLA Modules:
  0.0 327.7 jit_solution(8756651777962308982)
XLA Ops:
  6.5 1.4 slice_bitcast_fusion.1.refs_1_.refs_3_.refs_2_
  7.9 2.1 collective-permute-start
  10.1 1.0 collective-permute-start.1
  11.1 0.7 dynamic-slice_bitcast_fusion
  12.1 1.3 collective-permute-start.2
  13.6 1.2 collective-permute-start.4
  15.0 10.6 %collective-permute-done.2 = bf16[384,64]{0,1:T(8,128)(2,1)S(1)} collective-permute-done((bf16[384,64]{0,1:T(8,128)(2,1)S(1)}, bf16[384,64]{0,1:T(8,128)(2,1)S(1)}, u32[]{:S(2)}, u32[]{:S(2)}) %collective-permute-start.2) | collective-permute-done | bytes 49184 | tf_op jit(solution)/shard_map/ppermute | solution.py:320
  25.6 1.3 collective-permute-done.4
  27.2 1.2 collective-permute-start.6
  28.7 3.8 %bitcast_select_fusion = (bf16[256,1536]{1,0:T(8,128)(2,1)}, bf16[256,1536]{1,0:T(8,128)(2,1)}, bf16[256,1536]{1,0:T(8,128)(2,1)}, bf16[256,1536]{1,0:T(8,128)(2,1)}) fusion(bf16[4,1,256,1536]{3,2,1,0:T(8,128)(2,1)} %param.12, pred[256]{0:T(512)(128)(4,1)S(1)} %get-tuple-element.109, bf16[1536]{0:T(1024)(128)(2,1)S(1)} %copy-done.20, ...), kind=kLoop, calls=%fused_computation.2 | loop fusion | flops 1572864 | bytes 6295552 | tf_op jit(solution)/shard_map/jit(_where)/select_n | solution.py:410
  32.5 1.0 collective-permute-start.7
  33.6 8.8 %collective-permute-done.5.refs_3_.refs_5_.refs_4_ = bf16[192,3072]{1,0:T(8,128)(2,1)} collective-permute-done((bf16[192,3072]{1,0:T(8,128)(2,1)S(1)}, bf16[192,3072]{1,0:T(8,128)(2,1)}, u32[]{:S(2)}, u32[]{:S(2)}) %collective-permute-start.5) | collective-permute-done | bytes 1179680 | tf_op jit(solution)/shard_map/ppermute | solution.py:350
  42.4 1.2 collective-permute-start.9
  43.6 11.4 %collective-permute-done.6.refs_4_.refs_6_.refs_5_ = bf16[192,3072]{1,0:T(8,128)(2,1)} collective-permute-done((bf16[192,3072]{1,0:T(8,128)(2,1)}, bf16[192,3072]{1,0:T(8,128)(2,1)}, u32[]{:S(2)}, u32[]{:S(2)}) %collective-permute-start.6) | collective-permute-done | bytes 1179680 | tf_op jit(solution)/shard_map/ppermute | solution.py:349
  55.0 1.2 collective-permute-start.10
  56.3 0.7 transformed.2.refs_10_.refs_12_.refs_11_
  57.0 1.1 slice_bitcast_fusion
  58.1 0.9 collective-permute-done.10.refs_8_.refs_10_.refs_9_
  59.1 1.1 copy-done.8
  60.2 0.7 layer.12
  61.0 1.6 collective-permute-start.12
  62.5 0.7 collective-permute-start.11
  63.3 8.1 %collective-permute-done.12.refs_0_ = f32[8,128]{1,0:T(8,128)S(1)} collective-permute-done((f32[8,128]{1,0:T(8,128)S(1)}, f32[8,128]{1,0:T(8,128)S(1)}, u32[]{:S(2)}, u32[]{:S(2)}) %collective-permute-start.12) | collective-permute-done | bytes 4128 | tf_op jit(solution)/shard_map/ppermute | solution.py:459
  71.4 4.7 %targets.2.refs_13_.refs_1_ = bf16[4,256,768]{2,1,0:T(8,128)(2,1)S(1)} custom-call(s32[12,5]{1,0:T(8,128)S(1)} %and_select_fusion.flags, bf16[4,256,1536]{2,1,0:T(8,128)(2,1)S(1)} %bitcast.43, bf16[1536,768]{1,0:T(8,128)(2,1)S(1)} %copy-done.15, f32[8,128]{1,0:T(8,128)S(1)} %collective-permute-done.12.refs_0_), custom_call_target="tpu_custom_call" | custom-call | flops 2415919104 | bytes 5505024 | tf_op jit(solution)/shard_map/targets/pallas_call | solution.py:258
  76.1 9.1 %layer.13 = (bf16[256,1536]{1,0:T(8,128)(2,1)S(1)}, f32[8,128]{1,0:T(8,128)}) custom-call(s32[12,5]{1,0:T(8,128)S(1)} %and_select_fusion.flags, bf16[256,1536]{1,0:T(8,128)(2,1)S(1)} %copy-done.9, bf16[192,3072]{1,0:T(8,128)(2,1)S(1)} %slice_bitcast_fusion.1.refs_1_.refs_3_.refs_2_, bf16[192,3072]{1,0:T(8,128)(2,1)} %collective-permute-done.refs_2_.refs_4_.refs_3_, ...), custom_call_target="tpu_custom_call" | custom-call | flops 2415919104 | bytes 9437184 | tf_op jit(solution)/shard_map/layer/pallas_call | solution.py:190
  85.2 1.5 collective-permute-start.13
  86.7 9.2 %collective-permute-done.13.refs_2_ = bf16[256,1536]{1,0:T(8,128)(2,1)S(1)} collective-permute-done((bf16[256,1536]{1,0:T(8,128)(2,1)S(1)}, bf16[256,1536]{1,0:T(8,128)(2,1)S(1)}, u32[]{:S(2)}, u32[]{:S(2)}) %collective-permute-start.13) | collective-permute-done | bytes 786464 | tf_op jit(solution)/shard_map/ppermute | solution.py:449
  95.9 8.5 %layer.14 = (bf16[256,1536]{1,0:T(8,128)(2,1)S(1)}, f32[8,128]{1,0:T(8,128)S(1)}) custom-call(s32[12,5]{1,0:T(8,128)S(1)} %and_select_fusion.flags, bf16[256,1536]{1,0:T(8,128)(2,1)S(1)} %copy-done.10, bf16[256,1536]{1,0:T(8,128)(2,1)S(1)} %collective-permute-done.11.refs_1_, bf16[256,1536]{1,0:T(8,128)(2,1)S(1)} %collective-permute-done.13.refs_2_, ...), custom_call_target="tpu_custom_call" | custom-call | flops 2415919104 | bytes 9437184 | tf_op jit(solution)/shard_map/layer/pallas_call | solution.py:190
  104.4 4.3 %collective-permute-start.14 = (bf16[256,1536]{1,0:T(8,128)(2,1)S(1)}, bf16[256,1536]{1,0:T(8,128)(2,1)S(1)}, u32[]{:S(2)}, u32[]{:S(2)}) collective-permute-start(bf16[256,1536]{1,0:T(8,128)(2,1)S(1)} %get-tuple-element.84), channel_id=1, source_target_pairs={{0,8},{8,16},{1,9},{9,17},{2,10},{10,18},{3,11},{11,19},{4,12},{12... | collective-permute-start | bytes 2359304 | tf_op jit(solution)/shard_map/ppermute | solution.py:518
  108.7 1.4 collective-permute-start.15
  110.1 0.7 targets.3.refs_16_.tgt_ref
  110.8 8.7 %collective-permute-done.15.refs_15_ = s32[4,64,100]{2,1,0:T(8,128)S(1)} collective-permute-done((s32[4,64,100]{2,1,0:T(8,128)S(1)}, s32[4,64,100]{2,1,0:T(8,128)S(1)}, u32[]{:S(2)}, u32[]{:S(2)}) %collective-permute-start.15) | collective-permute-done | bytes 102432 | tf_op jit(solution)/shard_map/ppermute | solution.py:480
  119.6 8.7 %layer.15 = (bf16[256,1536]{1,0:T(8,128)(2,1)S(1)}, f32[8,128]{1,0:T(8,128)S(1)}) custom-call(s32[12,5]{1,0:T(8,128)S(1)} %and_select_fusion.flags, bf16[256,1536]{1,0:T(8,128)(2,1)S(1)} %copy-done.13, bf16[256,1536]{1,0:T(8,128)(2,1)S(1)} %collective-permute-done.14.refs_1_, bf16[192,3072]{1,0:T(8,128)(2,1)S(1)} %slice_bitcast_fusion.1.refs_1_.refs_3_.refs_2_, ...), custom_call_target="tpu_custom_call" | custom-call | flops 2415919104 | bytes 9437184 | tf_op jit(solution)/shard_map/layer/pallas_call | solution.py:190
  128.2 1.8 collective-permute-start.16
  130.8 8.2 %collective-permute-done.16.refs_1_ = bf16[256,1536]{1,0:T(8,128)(2,1)S(1)} collective-permute-done((bf16[256,1536]{1,0:T(8,128)(2,1)S(1)}, bf16[256,1536]{1,0:T(8,128)(2,1)S(1)}, u32[]{:S(2)}, u32[]{:S(2)}) %collective-permute-start.16) | collective-permute-done | bytes 786464 | tf_op jit(solution)/shard_map/ppermute | solution.py:518
  139.0 9.4 %layer.16 = (bf16[256,1536]{1,0:T(8,128)(2,1)}, f32[8,128]{1,0:T(8,128)S(1)}) custom-call(s32[12,5]{1,0:T(8,128)S(1)} %and_select_fusion.flags, bf16[256,1536]{1,0:T(8,128)(2,1)S(1)} %copy-done.12, bf16[256,1536]{1,0:T(8,128)(2,1)S(1)} %collective-permute-done.16.refs_1_, bf16[192,3072]{1,0:T(8,128)(2,1)S(1)} %slice_bitcast_fusion.1.refs_1_.refs_3_.refs_2_, ...), custom_call_target="tpu_custom_call" | custom-call | flops 2415919104 | bytes 9437184 | tf_op jit(solution)/shard_map/layer/pallas_call | solution.py:190
  148.4 2.0 collective-permute-start.18
  151.0 0.7 transformed.3.refs_12_.refs_13_.refs_3_
  151.7 1.1 copy-done.1
  152.8 9.5 %collective-permute-done.18.refs_0_ = bf16[256,1536]{1,0:T(8,128)(2,1)S(1)} collective-permute-done((bf16[256,1536]{1,0:T(8,128)(2,1)}, bf16[256,1536]{1,0:T(8,128)(2,1)S(1)}, u32[]{:S(2)}, u32[]{:S(2)}) %collective-permute-start.18) | collective-permute-done | bytes 786464 | tf_op jit(solution)/shard_map/ppermute | solution.py:518
  162.4 10.0 %layer.17 = (bf16[256,1536]{1,0:T(8,128)(2,1)S(1)}, f32[8,128]{1,0:T(8,128)}) custom-call(s32[12,5]{1,0:T(8,128)S(1)} %and_select_fusion.flags, bf16[256,1536]{1,0:T(8,128)(2,1)S(1)} %collective-permute-done.18.refs_0_, bf16[192,3072]{1,0:T(8,128)(2,1)S(1)} %slice_bitcast_fusion.1.refs_1_.refs_3_.refs_2_, ...), custom_call_target="tpu_custom_call" | custom-call | flops 2415919104 | bytes 9437184 | tf_op jit(solution)/shard_map/layer/pallas_call | solution.py:190
  172.4 12.6 %collective-permute-done.20.refs_0_ = bf16[256,1536]{1,0:T(8,128)(2,1)S(1)} collective-permute-done((bf16[256,1536]{1,0:T(8,128)(2,1)S(1)}, bf16[256,1536]{1,0:T(8,128)(2,1)S(1)}, u32[]{:S(2)}, u32[]{:S(2)}) %collective-permute-start.20) | collective-permute-done | bytes 786464 | tf_op jit(solution)/shard_map/ppermute | solution.py:518
  185.0 9.9 %layer.18 = (bf16[256,1536]{1,0:T(8,128)(2,1)S(1)}, f32[8,128]{1,0:T(8,128)}) custom-call(s32[12,5]{1,0:T(8,128)S(1)} %and_select_fusion.flags, bf16[256,1536]{1,0:T(8,128)(2,1)S(1)} %collective-permute-done.20.refs_0_, bf16[192,3072]{1,0:T(8,128)(2,1)S(1)} %slice_bitcast_fusion.1.refs_1_.refs_3_.refs_2_, ...), custom_call_target="tpu_custom_call" | custom-call | flops 2415919104 | bytes 9437184 | tf_op jit(solution)/shard_map/layer/pallas_call | solution.py:190
  194.9 0.7 collective-permute-start.21
  195.7 1.4 collective-permute-start.22
  197.1 6.7 %collective-permute-done.22.refs_16_ = bf16[16,128]{1,0:T(8,128)(2,1)S(1)} collective-permute-done((bf16[16,128]{1,0:T(8,128)(2,1)S(1)}, bf16[16,128]{1,0:T(8,128)(2,1)S(1)}, u32[]{:S(2)}, u32[]{:S(2)}) %collective-permute-start.22) | collective-permute-done | bytes 4128 | tf_op jit(solution)/shard_map/ppermute | solution.py:512
  203.8 1.9 collective-permute-start.23
  205.8 12.6 %collective-permute-done.23.refs_1_ = bf16[256,1536]{1,0:T(8,128)(2,1)S(1)} collective-permute-done((bf16[256,1536]{1,0:T(8,128)(2,1)S(1)}, bf16[256,1536]{1,0:T(8,128)(2,1)S(1)}, u32[]{:S(2)}, u32[]{:S(2)}) %collective-permute-start.23) | collective-permute-done | bytes 786464 | tf_op jit(solution)/shard_map/ppermute | solution.py:449
  218.4 10.0 %layer.19 = (bf16[256,1536]{1,0:T(8,128)(2,1)S(1)}, f32[8,128]{1,0:T(8,128)}) custom-call(s32[12,5]{1,0:T(8,128)S(1)} %and_select_fusion.flags, bf16[256,1536]{1,0:T(8,128)(2,1)S(1)} %collective-permute-done.21.refs_0_, bf16[256,1536]{1,0:T(8,128)(2,1)S(1)} %collective-permute-done.23.refs_1_, ...), custom_call_target="tpu_custom_call" | custom-call | flops 2415919104 | bytes 9437184 | tf_op jit(solution)/shard_map/layer/pallas_call | solution.py:190
  228.4 12.6 %collective-permute-done.24.refs_0_ = bf16[256,1536]{1,0:T(8,128)(2,1)S(1)} collective-permute-done((bf16[256,1536]{1,0:T(8,128)(2,1)S(1)}, bf16[256,1536]{1,0:T(8,128)(2,1)S(1)}, u32[]{:S(2)}, u32[]{:S(2)}) %collective-permute-start.24) | collective-permute-done | bytes 786464 | tf_op jit(solution)/shard_map/ppermute | solution.py:518
  241.0 8.7 %layer.20 = (bf16[256,1536]{1,0:T(8,128)(2,1)S(1)}, f32[8,128]{1,0:T(8,128)}) custom-call(s32[12,5]{1,0:T(8,128)S(1)} %and_select_fusion.flags, bf16[256,1536]{1,0:T(8,128)(2,1)S(1)} %collective-permute-done.24.refs_0_, bf16[1536,3072]{1,0:T(8,128)(2,1)} %all-gather.2.cloned.1.call-done.refs_9_.refs_10_.refs_1_, ...), custom_call_target="tpu_custom_call" | custom-call | flops 2415919104 | bytes 9437184 | tf_op jit(solution)/shard_map/layer/pallas_call | solution.py:190
  249.7 1.3 collective-permute-start.25
  251.1 8.9 %collective-permute-done.25.refs_0_ = bf16[256,1536]{1,0:T(8,128)(2,1)S(1)} collective-permute-done((bf16[256,1536]{1,0:T(8,128)(2,1)S(1)}, bf16[256,1536]{1,0:T(8,128)(2,1)S(1)}, u32[]{:S(2)}, u32[]{:S(2)}) %collective-permute-start.25) | collective-permute-done | bytes 786464 | tf_op jit(solution)/shard_map/ppermute | solution.py:518
  259.9 1.5 layer.21
  261.5 0.7 collective-permute-start.26
  262.2 1.3 layer.22
  263.6 0.8 collective-permute-start.27
  265.0 0.7 loss.4
  265.7 0.7 loss.5
  266.4 0.7 loss.6
  267.1 1.3 layer.23
  268.4 0.7 loss.7
  269.9 1.3 collective-permute-start.28
  271.9 48.3 %collective-permute-done.28 = f32[4,64]{1,0:T(4,128)S(1)} collective-permute-done((f32[4,64]{1,0:T(4,128)S(1)}, f32[4,64]{1,0:T(4,128)S(1)}, u32[]{:S(2)}, u32[]{:S(2)}) %collective-permute-start.28) | collective-permute-done | bytes 1056 | tf_op jit(solution)/shard_map/ppermute | solution.py:528
  (91 shorter events, 5.6 us)
Async XLA Ops:
  6.5 3.5 %copy-start.18 = (bf16[2,1,31,192]{3,0,2,1:T(2,128)(2,1)S(1)}, bf16[2,1,31,192]{3,0,2,1:T(2,128)(2,1)}, u32[]{:S(2)}) copy-start(bf16[2,1,31,192]{3,0,2,1:T(2,128)(2,1)} %param.14) | copy-start | bytes 71428
  6.5 8.3 %copy-start.19 = (s32[4,1,12]{2,1,0:T(1,128)S(1)}, s32[4,1,12]{2,1,0:T(1,128)}, u32[]{:S(2)}) copy-start(s32[4,1,12]{2,1,0:T(1,128)} %param.18) | copy-start | bytes 580
  6.5 22.2 %copy-start.20 = (bf16[1536]{0:T(1024)(128)(2,1)S(1)}, bf16[1536]{0:T(1024)(128)(2,1)}, u32[]{:S(2)}) copy-start(bf16[1536]{0:T(1024)(128)(2,1)} %param.15) | copy-start | bytes 9220
  6.5 144.5 %all-gather.2.cloned.1.call-start = ((), (), s32[]{:S(2)}) async-start(), calls=%async_computation | async-start | bytes 10616832 | tf_op jit(solution)/shard_map/all_gather | solution.py:453
  7.9 19.0 %collective-permute-start = (bf16[192,3072]{1,0:T(8,128)(2,1)S(1)}, bf16[192,3072]{1,0:T(8,128)(2,1)}, u32[]{:S(2)}, u32[]{:S(2)}) collective-permute-start(bf16[192,3072]{1,0:T(8,128)(2,1)S(1)} %slice_bitcast_fusion.1.refs_1_.refs_3_.refs_2_), channel_id=1, source_target_pairs={{0,4},{1,3},{2,6},{3,1},{4,0},{5,7},{6,2},{7,5},{8,12},{9,11},{10,... | collective-permute-start | bytes 3538952 | tf_op jit(solution)/shard_map/ppermute | solution.py:347
  10.1 1.9 collective-permute-start.1
  12.1 13.5 %collective-permute-start.2 = (bf16[384,64]{0,1:T(8,128)(2,1)S(1)}, bf16[384,64]{0,1:T(8,128)(2,1)S(1)}, u32[]{:S(2)}, u32[]{:S(2)}) collective-permute-start(bf16[384,64]{0,1:T(8,128)(2,1)S(1)} %pad_maximum_fusion.1), channel_id=1, source_target_pairs={{0,2},{1,3},{2,0},{3,1},{4,6},{5,7},{6,4},{7,5},{8,10},{9,11},{10,... | collective-permute-start | bytes 147464 | tf_op jit(solution)/shard_map/ppermute | solution.py:320
  13.4 12.2 %collective-permute-start.3 = (bf16[384,64]{0,1:T(8,128)(2,1)S(1)}, bf16[384,64]{0,1:T(8,128)(2,1)S(1)}, u32[]{:S(2)}, u32[]{:S(2)}) collective-permute-start(bf16[384,64]{0,1:T(8,128)(2,1)S(1)} %pad_maximum_fusion.1), channel_id=1, source_target_pairs={{0,4},{1,5},{2,6},{3,7},{4,0},{5,1},{6,2},{7,3},{8,12},{9,13},{10,... | collective-permute-start | bytes 147464 | tf_op jit(solution)/shard_map/ppermute | solution.py:320
  13.6 13.3 %collective-permute-start.4 = (bf16[384,64]{0,1:T(8,128)(2,1)S(1)}, bf16[384,64]{0,1:T(8,128)(2,1)S(1)}, u32[]{:S(2)}, u32[]{:S(2)}) collective-permute-start(bf16[384,64]{0,1:T(8,128)(2,1)S(1)} %pad_maximum_fusion.1), channel_id=1, source_target_pairs={{0,6},{1,7},{2,4},{3,5},{4,2},{5,3},{6,0},{7,1},{8,14},{9,15},{10,... | collective-permute-start | bytes 147464 | tf_op jit(solution)/shard_map/ppermute | solution.py:320
  26.9 15.5 %collective-permute-start.5 = (bf16[192,3072]{1,0:T(8,128)(2,1)S(1)}, bf16[192,3072]{1,0:T(8,128)(2,1)}, u32[]{:S(2)}, u32[]{:S(2)}) collective-permute-start(bf16[192,3072]{1,0:T(8,128)(2,1)S(1)} %slice_bitcast_fusion.1.refs_1_.refs_3_.refs_2_), channel_id=1, source_target_pairs={{0,2},{1,5},{2,0},{3,7},{4,6},{5,1},{6,4},{7,3},{8,10},{9,13},{10,... | collective-permute-start | bytes 3538952 | tf_op jit(solution)/shard_map/ppermute | solution.py:350
  27.2 27.9 %collective-permute-start.6 = (bf16[192,3072]{1,0:T(8,128)(2,1)}, bf16[192,3072]{1,0:T(8,128)(2,1)}, u32[]{:S(2)}, u32[]{:S(2)}) collective-permute-start(bf16[192,3072]{1,0:T(8,128)(2,1)} %collective-permute-done.refs_2_.refs_4_.refs_3_), channel_id=1, source_target_pairs={{0,2},{1,5},{2,0},{3,7},{4,6},{5,1},{6,4},{7,3},{8,10},{9,13},{10,... | collective-permute-start | bytes 3538952 | tf_op jit(solution)/shard_map/ppermute | solution.py:349
  28.7 27.5 %copy-start.14 = (bf16[3,240,32]{2,1,0:T(8,128)(2,1)S(1)}, bf16[3,240,32]{2,1,0:T(8,128)(2,1)}, u32[]{:S(2)}) copy-start(bf16[3,240,32]{2,1,0:T(8,128)(2,1)} %constant.99.clone.m_ref) | copy-start | bytes 138244
  32.5 24.4 %copy-start.16 = (bf16[2,1,192,3072]{3,2,1,0:T(8,128)(2,1)S(1)}, bf16[2,1,192,3072]{3,2,1,0:T(8,128)(2,1)}, u32[]{:S(2)}) copy-start(bf16[2,1,192,3072]{3,2,1,0:T(8,128)(2,1)} %param.13) | copy-start | bytes 7077892
  32.5 25.6 %collective-permute-start.7 = (bf16[192,3072]{1,0:T(8,128)(2,1)S(1)}, bf16[192,3072]{1,0:T(8,128)(2,1)}, u32[]{:S(2)}, u32[]{:S(2)}) collective-permute-start(bf16[192,3072]{1,0:T(8,128)(2,1)S(1)} %slice_bitcast_fusion.1.refs_1_.refs_3_.refs_2_), channel_id=1, source_target_pairs={{0,1},{1,0},{2,3},{3,2},{4,5},{5,4},{6,7},{7,6},{8,9},{9,8},{10,11... | collective-permute-start | bytes 3538952 | tf_op jit(solution)/shard_map/ppermute | solution.py:320
  33.5 24.6 %collective-permute-start.8 = (bf16[192,3072]{1,0:T(8,128)(2,1)}, bf16[192,3072]{1,0:T(8,128)(2,1)}, u32[]{:S(2)}, u32[]{:S(2)}) collective-permute-start(bf16[192,3072]{1,0:T(8,128)(2,1)} %collective-permute-done.refs_2_.refs_4_.refs_3_), channel_id=1, source_target_pairs={{0,1},{1,0},{2,3},{3,2},{4,5},{5,4},{6,7},{7,6},{8,9},{9,8},{10,11... | collective-permute-start | bytes 3538952 | tf_op jit(solution)/shard_map/ppermute | solution.py:320
  42.4 15.7 %collective-permute-start.9 = (bf16[192,3072]{1,0:T(8,128)(2,1)}, bf16[192,3072]{1,0:T(8,128)(2,1)}, u32[]{:S(2)}, u32[]{:S(2)}) collective-permute-start(bf16[192,3072]{1,0:T(8,128)(2,1)} %collective-permute-done.5.refs_3_.refs_5_.refs_4_), channel_id=1, source_target_pairs={{0,1},{1,0},{2,3},{3,2},{4,5},{5,4},{6,7},{7,6},{8,9},{9,8},{10,11... | collective-permute-start | bytes 3538952 | tf_op jit(solution)/shard_map/ppermute | solution.py:320
  55.0 4.0 %collective-permute-start.10 = (bf16[192,3072]{1,0:T(8,128)(2,1)}, bf16[192,3072]{1,0:T(8,128)(2,1)}, u32[]{:S(2)}, u32[]{:S(2)}) collective-permute-start(bf16[192,3072]{1,0:T(8,128)(2,1)} %collective-permute-done.6.refs_4_.refs_6_.refs_5_), channel_id=1, source_target_pairs={{0,1},{1,0},{2,3},{3,2},{4,5},{5,4},{6,7},{7,6},{8,9},{9,8},{10,11... | collective-permute-start | bytes 3538952 | tf_op jit(solution)/shard_map/ppermute | solution.py:320
  57.0 82.0 %copy-start = (f32[240,1536]{1,0:T(8,128)}, f32[240,1536]{1,0:T(8,128)S(1)}, u32[]{:S(2)}) copy-start(f32[240,1536]{1,0:T(8,128)S(1)} %transformed.2.refs_10_.refs_12_.refs_11_) | copy-start | bytes 4423684
  57.0 2.1 copy-start.6
  57.0 2.1 copy-start.7
  59.1 1.1 copy-start.8
  60.2 11.2 %copy-start.11 = (bf16[4,1,256,1536]{3,2,1,0:T(8,128)(2,1)S(1)}, bf16[4,1,256,1536]{3,2,1,0:T(8,128)(2,1)}, u32[]{:S(2)}) copy-start(bf16[4,1,256,1536]{3,2,1,0:T(8,128)(2,1)} %param.12) | copy-start | bytes 9437188
  60.2 11.2 %copy-start.15 = (bf16[1536,768]{1,0:T(8,128)(2,1)S(1)}, bf16[1536,768]{1,0:T(8,128)(2,1)}, u32[]{:S(2)}) copy-start(bf16[1536,768]{1,0:T(8,128)(2,1)} %w_tgt.3) | copy-start | bytes 7077892
  61.0 10.4 %collective-permute-start.12 = (f32[8,128]{1,0:T(8,128)S(1)}, f32[8,128]{1,0:T(8,128)S(1)}, u32[]{:S(2)}, u32[]{:S(2)}) collective-permute-start(f32[8,128]{1,0:T(8,128)S(1)} %get-tuple-element.82), channel_id=1, source_target_pairs={{0,1},{2,3},{4,5},{6,7},{8,9},{10,11},{12,13},{14,15},{16,17},{18,... | collective-permute-start | bytes 12296 | tf_op jit(solution)/shard_map/ppermute | solution.py:459
  62.5 24.1 %collective-permute-start.11 = (bf16[256,1536]{1,0:T(8,128)(2,1)S(1)}, bf16[256,1536]{1,0:T(8,128)(2,1)S(1)}, u32[]{:S(2)}, u32[]{:S(2)}) collective-permute-start(bf16[256,1536]{1,0:T(8,128)(2,1)S(1)} %get-tuple-element.81), channel_id=1, source_target_pairs={{0,8},{2,10},{4,12},{6,14}} | collective-permute-start | bytes 2359304 | tf_op jit(solution)/shard_map/ppermute | solution.py:449
  71.4 4.7 %copy-start.9 = (bf16[256,1536]{1,0:T(8,128)(2,1)S(1)}, bf16[256,1536]{1,0:T(8,128)(2,1)}, u32[]{:S(2)}) copy-start(bf16[256,1536]{1,0:T(8,128)(2,1)} %get-tuple-element.68.refs_0_) | copy-start | bytes 2359300
  76.1 19.8 %copy-start.10 = (bf16[256,1536]{1,0:T(8,128)(2,1)S(1)}, bf16[256,1536]{1,0:T(8,128)(2,1)}, u32[]{:S(2)}) copy-start(bf16[256,1536]{1,0:T(8,128)(2,1)} %get-tuple-element.67.refs_0_) | copy-start | bytes 2359300
  85.2 23.5 %copy-start.17 = (s32[4,1,64,100]{3,2,1,0:T(8,128)S(1)}, s32[4,1,64,100]{3,2,1,0:T(8,128)}, u32[]{:S(2)}) copy-start(s32[4,1,64,100]{3,2,1,0:T(8,128)} %param.19) | copy-start | bytes 307204
  85.2 10.7 %collective-permute-start.13 = (bf16[256,1536]{1,0:T(8,128)(2,1)S(1)}, bf16[256,1536]{1,0:T(8,128)(2,1)S(1)}, u32[]{:S(2)}, u32[]{:S(2)}) collective-permute-start(bf16[256,1536]{1,0:T(8,128)(2,1)S(1)} %get-tuple-element.83), channel_id=1, source_target_pairs={{1,9},{3,11},{5,13},{7,15}} | collective-permute-start | bytes 2359304 | tf_op jit(solution)/shard_map/ppermute | solution.py:449
  104.4 15.2 %collective-permute-start.14 = (bf16[256,1536]{1,0:T(8,128)(2,1)S(1)}, bf16[256,1536]{1,0:T(8,128)(2,1)S(1)}, u32[]{:S(2)}, u32[]{:S(2)}) collective-permute-start(bf16[256,1536]{1,0:T(8,128)(2,1)S(1)} %get-tuple-element.84), channel_id=1, source_target_pairs={{0,8},{8,16},{1,9},{9,17},{2,10},{10,18},{3,11},{11,19},{4,12},{12... | collective-permute-start | bytes 2359304 | tf_op jit(solution)/shard_map/ppermute | solution.py:518
  108.7 10.9 %copy-start.13 = (bf16[256,1536]{1,0:T(8,128)(2,1)S(1)}, bf16[256,1536]{1,0:T(8,128)(2,1)}, u32[]{:S(2)}) copy-start(bf16[256,1536]{1,0:T(8,128)(2,1)} %get-tuple-element.66.refs_0_) | copy-start | bytes 2359300
  108.7 10.9 %collective-permute-start.15 = (s32[4,64,100]{2,1,0:T(8,128)S(1)}, s32[4,64,100]{2,1,0:T(8,128)S(1)}, u32[]{:S(2)}, u32[]{:S(2)}) collective-permute-start(s32[4,64,100]{2,1,0:T(8,128)S(1)} %bitcast.48), channel_id=1, source_target_pairs={{0,24},{1,25},{2,26},{3,27},{4,28},{5,29},{6,30},{7,31}} | collective-permute-start | bytes 307208 | tf_op jit(solution)/shard_map/ppermute | solution.py:480
  110.8 17.4 %copy-start.3 = (bf16[4,256,768]{2,1,0:T(8,128)(2,1)}, bf16[4,256,768]{2,1,0:T(8,128)(2,1)S(1)}, u32[]{:S(2)}) copy-start(bf16[4,256,768]{2,1,0:T(8,128)(2,1)S(1)} %targets.3.refs_16_.tgt_ref) | copy-start | bytes 4718596
  110.8 28.1 %copy-start.12 = (bf16[256,1536]{1,0:T(8,128)(2,1)S(1)}, bf16[256,1536]{1,0:T(8,128)(2,1)}, u32[]{:S(2)}) copy-start(bf16[256,1536]{1,0:T(8,128)(2,1)} %get-tuple-element.65.refs_0_) | copy-start | bytes 2359300
  128.2 10.7 %collective-permute-start.16 = (bf16[256,1536]{1,0:T(8,128)(2,1)S(1)}, bf16[256,1536]{1,0:T(8,128)(2,1)S(1)}, u32[]{:S(2)}, u32[]{:S(2)}) collective-permute-start(bf16[256,1536]{1,0:T(8,128)(2,1)S(1)} %get-tuple-element.88), channel_id=1, source_target_pairs={{0,8},{8,16},{16,24},{1,9},{9,17},{17,25},{2,10},{10,18},{18,26},{... | collective-permute-start | bytes 2359304 | tf_op jit(solution)/shard_map/ppermute | solution.py:518
  130.1 0.7 collective-permute-start.17
  148.4 14.0 %collective-permute-start.18 = (bf16[256,1536]{1,0:T(8,128)(2,1)}, bf16[256,1536]{1,0:T(8,128)(2,1)S(1)}, u32[]{:S(2)}, u32[]{:S(2)}) collective-permute-start(bf16[256,1536]{1,0:T(8,128)(2,1)} %get-tuple-element.92), channel_id=1, source_target_pairs={{0,8},{8,16},{16,24},{24,0},{1,9},{9,17},{17,25},{25,1},{2,10},{10... | collective-permute-start | bytes 2359304 | tf_op jit(solution)/shard_map/ppermute | solution.py:518
  150.3 2.5 collective-permute-start.19
  151.7 1.1 copy-start.1
  172.3 12.7 %collective-permute-start.20 = (bf16[256,1536]{1,0:T(8,128)(2,1)S(1)}, bf16[256,1536]{1,0:T(8,128)(2,1)S(1)}, u32[]{:S(2)}, u32[]{:S(2)}) collective-permute-start(bf16[256,1536]{1,0:T(8,128)(2,1)S(1)} %get-tuple-element.100), channel_id=1, source_target_pairs={{0,8},{8,16},{16,24},{24,0},{1,9},{9,17},{17,25},{25,1},{2,10},{10... | collective-permute-start | bytes 2359304 | tf_op jit(solution)/shard_map/ppermute | solution.py:518
  194.9 0.7 collective-permute-start.21
  195.7 45.4 %copy-start.2 = (f32[240,1536]{1,0:T(8,128)S(1)}, f32[240,1536]{1,0:T(8,128)}, u32[]{:S(2)}) copy-start(f32[240,1536]{1,0:T(8,128)} %copy-done.1) | copy-start | bytes 4423684
  195.7 8.1 %collective-permute-start.22 = (bf16[16,128]{1,0:T(8,128)(2,1)S(1)}, bf16[16,128]{1,0:T(8,128)(2,1)S(1)}, u32[]{:S(2)}, u32[]{:S(2)}) collective-permute-start(bf16[16,128]{1,0:T(8,128)(2,1)S(1)} %slice.78), channel_id=1, source_target_pairs={{0,1},{2,3},{4,5},{6,7},{8,9},{10,11},{12,13},{14,15},{16,17},{18,... | collective-permute-start | bytes 12296 | tf_op jit(solution)/shard_map/ppermute | solution.py:512
  203.8 14.5 %collective-permute-start.23 = (bf16[256,1536]{1,0:T(8,128)(2,1)S(1)}, bf16[256,1536]{1,0:T(8,128)(2,1)S(1)}, u32[]{:S(2)}, u32[]{:S(2)}) collective-permute-start(bf16[256,1536]{1,0:T(8,128)(2,1)S(1)} %get-tuple-element.102), channel_id=1, source_target_pairs={{1,9},{3,11},{5,13},{7,15},{9,17},{11,19},{13,21},{15,23},{17,25},... | collective-permute-start | bytes 2359304 | tf_op jit(solution)/shard_map/ppermute | solution.py:449
  228.3 12.7 %collective-permute-start.24 = (bf16[256,1536]{1,0:T(8,128)(2,1)S(1)}, bf16[256,1536]{1,0:T(8,128)(2,1)S(1)}, u32[]{:S(2)}, u32[]{:S(2)}) collective-permute-start(bf16[256,1536]{1,0:T(8,128)(2,1)S(1)} %get-tuple-element.104), channel_id=1, source_target_pairs={{0,8},{8,16},{16,24},{24,0},{1,9},{9,17},{17,25},{25,1},{2,10},{10... | collective-permute-start | bytes 2359304 | tf_op jit(solution)/shard_map/ppermute | solution.py:518
  249.7 10.2 %collective-permute-start.25 = (bf16[256,1536]{1,0:T(8,128)(2,1)S(1)}, bf16[256,1536]{1,0:T(8,128)(2,1)S(1)}, u32[]{:S(2)}, u32[]{:S(2)}) collective-permute-start(bf16[256,1536]{1,0:T(8,128)(2,1)S(1)} %get-tuple-element.105.x_ref), channel_id=1, source_target_pairs={{0,8},{8,16},{16,24},{1,9},{9,17},{17,25},{2,10},{10,18},{18,26},{... | collective-permute-start | bytes 2359304 | tf_op jit(solution)/shard_map/ppermute | solution.py:518
  261.5 0.7 collective-permute-start.26
  262.2 2.3 copy-start.5
  263.6 1.5 copy-start.4
  263.6 3.5 %collective-permute-start.27 = (bf16[256,1536]{1,0:T(8,128)(2,1)S(1)}, bf16[256,1536]{1,0:T(8,128)(2,1)S(1)}, u32[]{:S(2)}, u32[]{:S(2)}) collective-permute-start(bf16[256,1536]{1,0:T(8,128)(2,1)S(1)} %get-tuple-element.107.x_ref), channel_id=1, source_target_pairs={{16,24},{17,25},{18,26},{19,27},{20,28},{21,29},{22,30},{23,31}} | collective-permute-start | bytes 2359304 | tf_op jit(solution)/shard_map/ppermute | solution.py:518
  269.2 2.6 collective-permute-start.30
  269.9 50.3 %collective-permute-start.28 = (f32[4,64]{1,0:T(4,128)S(1)}, f32[4,64]{1,0:T(4,128)S(1)}, u32[]{:S(2)}, u32[]{:S(2)}) collective-permute-start(f32[4,64]{1,0:T(4,128)S(1)} %get-tuple-element.127), channel_id=1, source_target_pairs={{24,0},{25,1},{26,2},{27,3},{28,4},{29,5},{30,6},{31,7}} | collective-permute-start | bytes 3080 | tf_op jit(solution)/shard_map/ppermute | solution.py:528
  271.2 49.0 %collective-permute-start.29 = (f32[4,64]{1,0:T(4,128)S(1)}, f32[4,64]{1,0:T(4,128)S(1)}, u32[]{:S(2)}, u32[]{:S(2)}) collective-permute-start(f32[4,64]{1,0:T(4,128)S(1)} %get-tuple-element.125), channel_id=1, source_target_pairs={{24,8},{25,9},{26,10},{27,11},{28,12},{29,13},{30,14},{31,15}} | collective-permute-start | bytes 3080 | tf_op jit(solution)/shard_map/ppermute | solution.py:528
Sparse Core Ops, SparseCore 0:
  59.2 60.7 all-gather.1
where the time goes:
time: 328 us
  waiting for transfers between devices  179 us (55%)
  Pallas kernels  88.6 us (27%)
  starting transfers between devices  35 us (11%)
  between operations  14.1 us (4%)
  local copies, waits for them, and re-layouts  6.54 us (2%)
  other arithmetic  4.86 us (1%)
    pallas_call x12, Pallas kernels, layer(): pl.pallas_call(functools.partial(layer_body, entry, kinds, fresh_slot, le...  79.1 us
    ppermute x8, waiting for transfers between devices, on_device(): state = [lax.ppermute(result, 'section', route)]  51.8 us
    ppermute x3, waiting for transfers between devices, on_device(): mine = mine + lax.ppermute(cut, 'section', [(last, s)])  48.3 us
    ppermute x4, waiting for transfers between devices, hop_of(): return lax.ppermute(block, ('section', 'fsdp'), route)  21.8 us
    ppermute x8, waiting for transfers between devices, swap(): lax.ppermute(block, axis, [(i, i ^ mask) for i in range(lax.axis_size(axi...  12.9 us
    ppermute x1, waiting for transfers between devices, crossed(): far = lax.ppermute(near, axis, other)  11.4 us
    ppermute x8, starting transfers between devices, on_device(): state = [lax.ppermute(result, 'section', route)]  11.1 us
    ppermute x1, waiting for transfers between devices, crossed(): side = lax.ppermute(block, axis, other)  8.76 us
  transfers between devices with their start and end apart: 32, of which 16 were waited for; matrix products, arithmetic and copies ran while one was open for 2% of the time, Pallas kernels for 14%

commit v1 on v0

--- a/solution.py
+++ b/solution.py
@@ -113,7 +113,7 @@
 
     @pl.when(valid == 1)
     def _():
-        ahead = min(3, chunks)
+        ahead = min(2, chunks)
         if x_sem is not None:
             options = ([] if fresh is None else [fresh]) + recv
             first = base

time: 328 us -> 348 us (1.061)
  Pallas kernels: 88.6 us -> 102 us
  waiting for transfers between devices: 179 us -> 184 us
    pallas_call x12, Pallas kernels: 79.1 us -> 92.1 us  [layer(): pl.pallas_call(functools.partial(layer_body, entry, kinds, fresh_slot, le...]
    ppermute x3, waiting for transfers between devices: 48.3 us -> 53.4 us  [on_device(): mine = mine + lax.ppermute(cut, 'section', [(last, s)])]
  transfers between devices with their start and end apart: 32 -> 32, of which waited for: 16 -> 16; matrix products, arithmetic and copies ran while one was open for 2% -> 2% of each run, Pallas kernels for 14% -> 15%
where the time goes in v1:
time: 348 us; the launch traced here: 346 us
  waiting for transfers between devices  184 us (53%)
  Pallas kernels  102 us (29%)
  starting transfers between devices  35.4 us (10%)
  between operations  14.1 us (4%)
  local copies, waits for them, and re-layouts  6.54 us (2%)
  other arithmetic  4.86 us (1%)
    pallas_call x12, Pallas kernels, layer(): pl.pallas_call(functools.partial(layer_body, entry, kinds, fresh_slot, le...  92.1 us
    ppermute x3, waiting for transfers between devices, on_device(): mine = mine + lax.ppermute(cut, 'section', [(last, s)])  53.4 us
    ppermute x8, waiting for transfers between devices, on_device(): state = [lax.ppermute(result, 'section', route)]  51.4 us
    ppermute x4, waiting for transfers between devices, hop_of(): return lax.ppermute(block, ('section', 'fsdp'), route)  21.5 us
    ppermute x8, waiting for transfers between devices, swap(): lax.ppermute(block, axis, [(i, i ^ mask) for i in range(lax.axis_size(axi...  12.9 us
    ppermute x8, starting transfers between devices, on_device(): state = [lax.ppermute(result, 'section', route)]  11.5 us
    ppermute x1, waiting for transfers between devices, crossed(): far = lax.ppermute(near, axis, other)  11.4 us
    ppermute x1, waiting for transfers between devices, on_device(): token = lax.ppermute(mark, 'fsdp', [(i, i + 1) for i in range(0, size, 2)])  10.1 us
  transfers between devices with their start and end apart: 32, of which 16 were waited for; matrix products, arithmetic and copies ran while one was open for 2% of the time, Pallas kernels for 15%

profile of v1, /device:TPU:1, one launch (start us, length us, event | category | flops | bytes accessed | tf_op | source)
XLA Modules:
  0.0 346.2 jit_solution(9283976698829468615)
XLA Ops:
  6.5 1.4 slice_bitcast_fusion.1.refs_1_.refs_3_.refs_2_
  7.9 2.1 collective-permute-start
  10.1 1.0 collective-permute-start.1
  11.1 0.7 dynamic-slice_bitcast_fusion
  12.1 1.3 collective-permute-start.2
  13.6 1.2 collective-permute-start.4
  15.0 10.6 %collective-permute-done.2 = bf16[384,64]{0,1:T(8,128)(2,1)S(1)} collective-permute-done((bf16[384,64]{0,1:T(8,128)(2,1)S(1)}, bf16[384,64]{0,1:T(8,128)(2,1)S(1)}, u32[]{:S(2)}, u32[]{:S(2)}) %collective-permute-start.2) | collective-permute-done | bytes 49184 | tf_op jit(solution)/shard_map/ppermute | solution.py:320
  25.6 1.3 collective-permute-done.4
  27.2 1.2 collective-permute-start.6
  28.7 3.8 %bitcast_select_fusion = (bf16[256,1536]{1,0:T(8,128)(2,1)}, bf16[256,1536]{1,0:T(8,128)(2,1)}, bf16[256,1536]{1,0:T(8,128)(2,1)}, bf16[256,1536]{1,0:T(8,128)(2,1)}) fusion(bf16[4,1,256,1536]{3,2,1,0:T(8,128)(2,1)} %param.12, pred[256]{0:T(512)(128)(4,1)S(1)} %get-tuple-element.109, bf16[1536]{0:T(1024)(128)(2,1)S(1)} %copy-done.20, ...), kind=kLoop, calls=%fused_computation.2 | loop fusion | flops 1572864 | bytes 6295552 | tf_op jit(solution)/shard_map/jit(_where)/select_n | solution.py:410
  32.5 1.0 collective-permute-start.7
  33.6 8.8 %collective-permute-done.5.refs_3_.refs_5_.refs_4_ = bf16[192,3072]{1,0:T(8,128)(2,1)} collective-permute-done((bf16[192,3072]{1,0:T(8,128)(2,1)S(1)}, bf16[192,3072]{1,0:T(8,128)(2,1)}, u32[]{:S(2)}, u32[]{:S(2)}) %collective-permute-start.5) | collective-permute-done | bytes 1179680 | tf_op jit(solution)/shard_map/ppermute | solution.py:350
  42.4 1.2 collective-permute-start.9
  43.6 11.4 %collective-permute-done.6.refs_4_.refs_6_.refs_5_ = bf16[192,3072]{1,0:T(8,128)(2,1)} collective-permute-done((bf16[192,3072]{1,0:T(8,128)(2,1)}, bf16[192,3072]{1,0:T(8,128)(2,1)}, u32[]{:S(2)}, u32[]{:S(2)}) %collective-permute-start.6) | collective-permute-done | bytes 1179680 | tf_op jit(solution)/shard_map/ppermute | solution.py:349
  55.0 1.2 collective-permute-start.10
  56.3 0.7 transformed.2.refs_10_.refs_12_.refs_11_
  57.0 1.1 slice_bitcast_fusion
  58.1 0.9 collective-permute-done.10.refs_8_.refs_10_.refs_9_
  59.1 1.1 copy-done.8
  60.2 0.7 layer.12
  61.0 1.6 collective-permute-start.12
  62.5 0.7 collective-permute-start.11
  63.3 10.1 %collective-permute-done.12.refs_0_ = f32[8,128]{1,0:T(8,128)S(1)} collective-permute-done((f32[8,128]{1,0:T(8,128)S(1)}, f32[8,128]{1,0:T(8,128)S(1)}, u32[]{:S(2)}, u32[]{:S(2)}) %collective-permute-start.12) | collective-permute-done | bytes 4128 | tf_op jit(solution)/shard_map/ppermute | solution.py:459
  73.4 4.7 %targets.2.refs_13_.refs_1_ = bf16[4,256,768]{2,1,0:T(8,128)(2,1)S(1)} custom-call(s32[12,5]{1,0:T(8,128)S(1)} %and_select_fusion.flags, bf16[4,256,1536]{2,1,0:T(8,128)(2,1)S(1)} %bitcast.43, bf16[1536,768]{1,0:T(8,128)(2,1)S(1)} %copy-done.15, f32[8,128]{1,0:T(8,128)S(1)} %collective-permute-done.12.refs_0_), custom_call_target="tpu_custom_call" | custom-call | flops 2415919104 | bytes 5505024 | tf_op jit(solution)/shard_map/targets/pallas_call | solution.py:258
  78.1 10.7 %layer.13 = (bf16[256,1536]{1,0:T(8,128)(2,1)S(1)}, f32[8,128]{1,0:T(8,128)}) custom-call(s32[12,5]{1,0:T(8,128)S(1)} %and_select_fusion.flags, bf16[256,1536]{1,0:T(8,128)(2,1)S(1)} %copy-done.9, bf16[192,3072]{1,0:T(8,128)(2,1)S(1)} %slice_bitcast_fusion.1.refs_1_.refs_3_.refs_2_, bf16[192,3072]{1,0:T(8,128)(2,1)} %collective-permute-done.refs_2_.refs_4_.refs_3_, ...), custom_call_target="tpu_custom_call" | custom-call | flops 2415919104 | bytes 9437184 | tf_op jit(solution)/shard_map/layer/pallas_call | solution.py:190
  88.7 1.5 collective-permute-start.13
  90.2 8.9 %collective-permute-done.13.refs_2_ = bf16[256,1536]{1,0:T(8,128)(2,1)S(1)} collective-permute-done((bf16[256,1536]{1,0:T(8,128)(2,1)S(1)}, bf16[256,1536]{1,0:T(8,128)(2,1)S(1)}, u32[]{:S(2)}, u32[]{:S(2)}) %collective-permute-start.13) | collective-permute-done | bytes 786464 | tf_op jit(solution)/shard_map/ppermute | solution.py:449
  99.1 10.2 %layer.14 = (bf16[256,1536]{1,0:T(8,128)(2,1)S(1)}, f32[8,128]{1,0:T(8,128)S(1)}) custom-call(s32[12,5]{1,0:T(8,128)S(1)} %and_select_fusion.flags, bf16[256,1536]{1,0:T(8,128)(2,1)S(1)} %copy-done.10, bf16[256,1536]{1,0:T(8,128)(2,1)S(1)} %collective-permute-done.11.refs_1_, bf16[256,1536]{1,0:T(8,128)(2,1)S(1)} %collective-permute-done.13.refs_2_, ...), custom_call_target="tpu_custom_call" | custom-call | flops 2415919104 | bytes 9437184 | tf_op jit(solution)/shard_map/layer/pallas_call | solution.py:190
  109.3 4.1 %collective-permute-start.14 = (bf16[256,1536]{1,0:T(8,128)(2,1)S(1)}, bf16[256,1536]{1,0:T(8,128)(2,1)S(1)}, u32[]{:S(2)}, u32[]{:S(2)}) collective-permute-start(bf16[256,1536]{1,0:T(8,128)(2,1)S(1)} %get-tuple-element.84), channel_id=1, source_target_pairs={{0,8},{8,16},{1,9},{9,17},{2,10},{10,18},{3,11},{11,19},{4,12},{12... | collective-permute-start | bytes 2359304 | tf_op jit(solution)/shard_map/ppermute | solution.py:518
  113.5 1.4 collective-permute-start.15
  114.9 0.7 targets.3.refs_16_.tgt_ref
  115.6 8.1 %collective-permute-done.15.refs_15_ = s32[4,64,100]{2,1,0:T(8,128)S(1)} collective-permute-done((s32[4,64,100]{2,1,0:T(8,128)S(1)}, s32[4,64,100]{2,1,0:T(8,128)S(1)}, u32[]{:S(2)}, u32[]{:S(2)}) %collective-permute-start.15) | collective-permute-done | bytes 102432 | tf_op jit(solution)/shard_map/ppermute | solution.py:480
  123.8 10.3 %layer.15 = (bf16[256,1536]{1,0:T(8,128)(2,1)S(1)}, f32[8,128]{1,0:T(8,128)S(1)}) custom-call(s32[12,5]{1,0:T(8,128)S(1)} %and_select_fusion.flags, bf16[256,1536]{1,0:T(8,128)(2,1)S(1)} %copy-done.13, bf16[256,1536]{1,0:T(8,128)(2,1)S(1)} %collective-permute-done.14.refs_1_, bf16[192,3072]{1,0:T(8,128)(2,1)S(1)} %slice_bitcast_fusion.1.refs_1_.refs_3_.refs_2_, ...), custom_call_target="tpu_custom_call" | custom-call | flops 2415919104 | bytes 9437184 | tf_op jit(solution)/shard_map/layer/pallas_call | solution.py:190
  134.1 2.4 collective-permute-start.16
  137.2 8.2 %collective-permute-done.16.refs_1_ = bf16[256,1536]{1,0:T(8,128)(2,1)S(1)} collective-permute-done((bf16[256,1536]{1,0:T(8,128)(2,1)S(1)}, bf16[256,1536]{1,0:T(8,128)(2,1)S(1)}, u32[]{:S(2)}, u32[]{:S(2)}) %collective-permute-start.16) | collective-permute-done | bytes 786464 | tf_op jit(solution)/shard_map/ppermute | solution.py:518
  145.3 11.0 %layer.16 = (bf16[256,1536]{1,0:T(8,128)(2,1)}, f32[8,128]{1,0:T(8,128)S(1)}) custom-call(s32[12,5]{1,0:T(8,128)S(1)} %and_select_fusion.flags, bf16[256,1536]{1,0:T(8,128)(2,1)S(1)} %copy-done.12, bf16[256,1536]{1,0:T(8,128)(2,1)S(1)} %collective-permute-done.16.refs_1_, bf16[192,3072]{1,0:T(8,128)(2,1)S(1)} %slice_bitcast_fusion.1.refs_1_.refs_3_.refs_2_, ...), custom_call_target="tpu_custom_call" | custom-call | flops 2415919104 | bytes 9437184 | tf_op jit(solution)/shard_map/layer/pallas_call | solution.py:190
  156.3 2.0 collective-permute-start.18
  159.0 0.7 transformed.3.refs_12_.refs_13_.refs_3_
  159.7 1.1 copy-done.1
  160.8 9.1 %collective-permute-done.18.refs_0_ = bf16[256,1536]{1,0:T(8,128)(2,1)S(1)} collective-permute-done((bf16[256,1536]{1,0:T(8,128)(2,1)}, bf16[256,1536]{1,0:T(8,128)(2,1)S(1)}, u32[]{:S(2)}, u32[]{:S(2)}) %collective-permute-start.18) | collective-permute-done | bytes 786464 | tf_op jit(solution)/shard_map/ppermute | solution.py:518
  169.9 11.6 %layer.17 = (bf16[256,1536]{1,0:T(8,128)(2,1)S(1)}, f32[8,128]{1,0:T(8,128)}) custom-call(s32[12,5]{1,0:T(8,128)S(1)} %and_select_fusion.flags, bf16[256,1536]{1,0:T(8,128)(2,1)S(1)} %collective-permute-done.18.refs_0_, bf16[192,3072]{1,0:T(8,128)(2,1)S(1)} %slice_bitcast_fusion.1.refs_1_.refs_3_.refs_2_, ...), custom_call_target="tpu_custom_call" | custom-call | flops 2415919104 | bytes 9437184 | tf_op jit(solution)/shard_map/layer/pallas_call | solution.py:190
  181.6 12.6 %collective-permute-done.20.refs_0_ = bf16[256,1536]{1,0:T(8,128)(2,1)S(1)} collective-permute-done((bf16[256,1536]{1,0:T(8,128)(2,1)S(1)}, bf16[256,1536]{1,0:T(8,128)(2,1)S(1)}, u32[]{:S(2)}, u32[]{:S(2)}) %collective-permute-start.20) | collective-permute-done | bytes 786464 | tf_op jit(solution)/shard_map/ppermute | solution.py:518
  194.2 11.5 %layer.18 = (bf16[256,1536]{1,0:T(8,128)(2,1)S(1)}, f32[8,128]{1,0:T(8,128)}) custom-call(s32[12,5]{1,0:T(8,128)S(1)} %and_select_fusion.flags, bf16[256,1536]{1,0:T(8,128)(2,1)S(1)} %collective-permute-done.20.refs_0_, bf16[192,3072]{1,0:T(8,128)(2,1)S(1)} %slice_bitcast_fusion.1.refs_1_.refs_3_.refs_2_, ...), custom_call_target="tpu_custom_call" | custom-call | flops 2415919104 | bytes 9437184 | tf_op jit(solution)/shard_map/layer/pallas_call | solution.py:190
  205.7 0.7 collective-permute-start.21
  206.5 1.4 collective-permute-start.22
  207.9 6.0 %collective-permute-done.22.refs_16_ = bf16[16,128]{1,0:T(8,128)(2,1)S(1)} collective-permute-done((bf16[16,128]{1,0:T(8,128)(2,1)S(1)}, bf16[16,128]{1,0:T(8,128)(2,1)S(1)}, u32[]{:S(2)}, u32[]{:S(2)}) %collective-permute-start.22) | collective-permute-done | bytes 4128 | tf_op jit(solution)/shard_map/ppermute | solution.py:512
  213.9 1.9 collective-permute-start.23
  215.8 12.6 %collective-permute-done.23.refs_1_ = bf16[256,1536]{1,0:T(8,128)(2,1)S(1)} collective-permute-done((bf16[256,1536]{1,0:T(8,128)(2,1)S(1)}, bf16[256,1536]{1,0:T(8,128)(2,1)S(1)}, u32[]{:S(2)}, u32[]{:S(2)}) %collective-permute-start.23) | collective-permute-done | bytes 786464 | tf_op jit(solution)/shard_map/ppermute | solution.py:449
  228.4 11.6 %layer.19 = (bf16[256,1536]{1,0:T(8,128)(2,1)S(1)}, f32[8,128]{1,0:T(8,128)}) custom-call(s32[12,5]{1,0:T(8,128)S(1)} %and_select_fusion.flags, bf16[256,1536]{1,0:T(8,128)(2,1)S(1)} %collective-permute-done.21.refs_0_, bf16[256,1536]{1,0:T(8,128)(2,1)S(1)} %collective-permute-done.23.refs_1_, ...), custom_call_target="tpu_custom_call" | custom-call | flops 2415919104 | bytes 9437184 | tf_op jit(solution)/shard_map/layer/pallas_call | solution.py:190
  240.1 12.6 %collective-permute-done.24.refs_0_ = bf16[256,1536]{1,0:T(8,128)(2,1)S(1)} collective-permute-done((bf16[256,1536]{1,0:T(8,128)(2,1)S(1)}, bf16[256,1536]{1,0:T(8,128)(2,1)S(1)}, u32[]{:S(2)}, u32[]{:S(2)}) %collective-permute-start.24) | collective-permute-done | bytes 786464 | tf_op jit(solution)/shard_map/ppermute | solution.py:518
  252.7 10.4 %layer.20 = (bf16[256,1536]{1,0:T(8,128)(2,1)S(1)}, f32[8,128]{1,0:T(8,128)}) custom-call(s32[12,5]{1,0:T(8,128)S(1)} %and_select_fusion.flags, bf16[256,1536]{1,0:T(8,128)(2,1)S(1)} %collective-permute-done.24.refs_0_, bf16[1536,3072]{1,0:T(8,128)(2,1)} %all-gather.2.cloned.1.call-done.refs_9_.refs_10_.refs_1_, ...), custom_call_target="tpu_custom_call" | custom-call | flops 2415919104 | bytes 9437184 | tf_op jit(solution)/shard_map/layer/pallas_call | solution.py:190
  263.1 1.3 collective-permute-start.25
  264.5 8.9 %collective-permute-done.25.refs_0_ = bf16[256,1536]{1,0:T(8,128)(2,1)S(1)} collective-permute-done((bf16[256,1536]{1,0:T(8,128)(2,1)S(1)}, bf16[256,1536]{1,0:T(8,128)(2,1)S(1)}, u32[]{:S(2)}, u32[]{:S(2)}) %collective-permute-start.25) | collective-permute-done | bytes 786464 | tf_op jit(solution)/shard_map/ppermute | solution.py:518
  273.3 1.5 layer.21
  274.9 0.7 collective-permute-start.26
  275.6 1.3 layer.22
  276.9 0.8 collective-permute-start.27
  278.4 0.7 loss.4
  279.1 0.7 loss.5
  279.8 0.7 loss.6
  280.5 1.3 layer.23
  281.8 0.7 loss.7
  283.2 1.3 collective-permute-start.28
  285.2 53.4 %collective-permute-done.28 = f32[4,64]{1,0:T(4,128)S(1)} collective-permute-done((f32[4,64]{1,0:T(4,128)S(1)}, f32[4,64]{1,0:T(4,128)S(1)}, u32[]{:S(2)}, u32[]{:S(2)}) %collective-permute-start.28) | collective-permute-done | bytes 1056 | tf_op jit(solution)/shard_map/ppermute | solution.py:528
  (91 shorter events, 5.6 us)
Async XLA Ops:
  6.5 3.5 %copy-start.18 = (bf16[2,1,31,192]{3,0,2,1:T(2,128)(2,1)S(1)}, bf16[2,1,31,192]{3,0,2,1:T(2,128)(2,1)}, u32[]{:S(2)}) copy-start(bf16[2,1,31,192]{3,0,2,1:T(2,128)(2,1)} %param.14) | copy-start | bytes 71428
  6.5 8.3 %copy-start.19 = (s32[4,1,12]{2,1,0:T(1,128)S(1)}, s32[4,1,12]{2,1,0:T(1,128)}, u32[]{:S(2)}) copy-start(s32[4,1,12]{2,1,0:T(1,128)} %param.18) | copy-start | bytes 580
  6.5 22.2 %copy-start.20 = (bf16[1536]{0:T(1024)(128)(2,1)S(1)}, bf16[1536]{0:T(1024)(128)(2,1)}, u32[]{:S(2)}) copy-start(bf16[1536]{0:T(1024)(128)(2,1)} %param.15) | copy-start | bytes 9220
  6.5 152.4 %all-gather.2.cloned.1.call-start = ((), (), s32[]{:S(2)}) async-start(), calls=%async_computation | async-start | bytes 10616832 | tf_op jit(solution)/shard_map/all_gather | solution.py:453
  7.9 19.0 %collective-permute-start = (bf16[192,3072]{1,0:T(8,128)(2,1)S(1)}, bf16[192,3072]{1,0:T(8,128)(2,1)}, u32[]{:S(2)}, u32[]{:S(2)}) collective-permute-start(bf16[192,3072]{1,0:T(8,128)(2,1)S(1)} %slice_bitcast_fusion.1.refs_1_.refs_3_.refs_2_), channel_id=1, source_target_pairs={{0,4},{1,3},{2,6},{3,1},{4,0},{5,7},{6,2},{7,5},{8,12},{9,11},{10,... | collective-permute-start | bytes 3538952 | tf_op jit(solution)/shard_map/ppermute | solution.py:347
  10.1 1.9 collective-permute-start.1
  12.1 13.5 %collective-permute-start.2 = (bf16[384,64]{0,1:T(8,128)(2,1)S(1)}, bf16[384,64]{0,1:T(8,128)(2,1)S(1)}, u32[]{:S(2)}, u32[]{:S(2)}) collective-permute-start(bf16[384,64]{0,1:T(8,128)(2,1)S(1)} %pad_maximum_fusion.1), channel_id=1, source_target_pairs={{0,2},{1,3},{2,0},{3,1},{4,6},{5,7},{6,4},{7,5},{8,10},{9,11},{10,... | collective-permute-start | bytes 147464 | tf_op jit(solution)/shard_map/ppermute | solution.py:320
  13.4 12.2 %collective-permute-start.3 = (bf16[384,64]{0,1:T(8,128)(2,1)S(1)}, bf16[384,64]{0,1:T(8,128)(2,1)S(1)}, u32[]{:S(2)}, u32[]{:S(2)}) collective-permute-start(bf16[384,64]{0,1:T(8,128)(2,1)S(1)} %pad_maximum_fusion.1), channel_id=1, source_target_pairs={{0,4},{1,5},{2,6},{3,7},{4,0},{5,1},{6,2},{7,3},{8,12},{9,13},{10,... | collective-permute-start | bytes 147464 | tf_op jit(solution)/shard_map/ppermute | solution.py:320
  13.6 13.3 %collective-permute-start.4 = (bf16[384,64]{0,1:T(8,128)(2,1)S(1)}, bf16[384,64]{0,1:T(8,128)(2,1)S(1)}, u32[]{:S(2)}, u32[]{:S(2)}) collective-permute-start(bf16[384,64]{0,1:T(8,128)(2,1)S(1)} %pad_maximum_fusion.1), channel_id=1, source_target_pairs={{0,6},{1,7},{2,4},{3,5},{4,2},{5,3},{6,0},{7,1},{8,14},{9,15},{10,... | collective-permute-start | bytes 147464 | tf_op jit(solution)/shard_map/ppermute | solution.py:320
  26.9 15.5 %collective-permute-start.5 = (bf16[192,3072]{1,0:T(8,128)(2,1)S(1)}, bf16[192,3072]{1,0:T(8,128)(2,1)}, u32[]{:S(2)}, u32[]{:S(2)}) collective-permute-start(bf16[192,3072]{1,0:T(8,128)(2,1)S(1)} %slice_bitcast_fusion.1.refs_1_.refs_3_.refs_2_), channel_id=1, source_target_pairs={{0,2},{1,5},{2,0},{3,7},{4,6},{5,1},{6,4},{7,3},{8,10},{9,13},{10,... | collective-permute-start | bytes 3538952 | tf_op jit(solution)/shard_map/ppermute | solution.py:350
  27.2 27.9 %collective-permute-start.6 = (bf16[192,3072]{1,0:T(8,128)(2,1)}, bf16[192,3072]{1,0:T(8,128)(2,1)}, u32[]{:S(2)}, u32[]{:S(2)}) collective-permute-start(bf16[192,3072]{1,0:T(8,128)(2,1)} %collective-permute-done.refs_2_.refs_4_.refs_3_), channel_id=1, source_target_pairs={{0,2},{1,5},{2,0},{3,7},{4,6},{5,1},{6,4},{7,3},{8,10},{9,13},{10,... | collective-permute-start | bytes 3538952 | tf_op jit(solution)/shard_map/ppermute | solution.py:349
  28.7 27.5 %copy-start.14 = (bf16[3,240,32]{2,1,0:T(8,128)(2,1)S(1)}, bf16[3,240,32]{2,1,0:T(8,128)(2,1)}, u32[]{:S(2)}) copy-start(bf16[3,240,32]{2,1,0:T(8,128)(2,1)} %constant.99.clone.m_ref) | copy-start | bytes 138244
  32.5 24.4 %copy-start.16 = (bf16[2,1,192,3072]{3,2,1,0:T(8,128)(2,1)S(1)}, bf16[2,1,192,3072]{3,2,1,0:T(8,128)(2,1)}, u32[]{:S(2)}) copy-start(bf16[2,1,192,3072]{3,2,1,0:T(8,128)(2,1)} %param.13) | copy-start | bytes 7077892
  32.5 25.6 %collective-permute-start.7 = (bf16[192,3072]{1,0:T(8,128)(2,1)S(1)}, bf16[192,3072]{1,0:T(8,128)(2,1)}, u32[]{:S(2)}, u32[]{:S(2)}) collective-permute-start(bf16[192,3072]{1,0:T(8,128)(2,1)S(1)} %slice_bitcast_fusion.1.refs_1_.refs_3_.refs_2_), channel_id=1, source_target_pairs={{0,1},{1,0},{2,3},{3,2},{4,5},{5,4},{6,7},{7,6},{8,9},{9,8},{10,11... | collective-permute-start | bytes 3538952 | tf_op jit(solution)/shard_map/ppermute | solution.py:320
  33.5 24.6 %collective-permute-start.8 = (bf16[192,3072]{1,0:T(8,128)(2,1)}, bf16[192,3072]{1,0:T(8,128)(2,1)}, u32[]{:S(2)}, u32[]{:S(2)}) collective-permute-start(bf16[192,3072]{1,0:T(8,128)(2,1)} %collective-permute-done.refs_2_.refs_4_.refs_3_), channel_id=1, source_target_pairs={{0,1},{1,0},{2,3},{3,2},{4,5},{5,4},{6,7},{7,6},{8,9},{9,8},{10,11... | collective-permute-start | bytes 3538952 | tf_op jit(solution)/shard_map/ppermute | solution.py:320
  42.4 15.7 %collective-permute-start.9 = (bf16[192,3072]{1,0:T(8,128)(2,1)}, bf16[192,3072]{1,0:T(8,128)(2,1)}, u32[]{:S(2)}, u32[]{:S(2)}) collective-permute-start(bf16[192,3072]{1,0:T(8,128)(2,1)} %collective-permute-done.5.refs_3_.refs_5_.refs_4_), channel_id=1, source_target_pairs={{0,1},{1,0},{2,3},{3,2},{4,5},{5,4},{6,7},{7,6},{8,9},{9,8},{10,11... | collective-permute-start | bytes 3538952 | tf_op jit(solution)/shard_map/ppermute | solution.py:320
  55.0 4.0 %collective-permute-start.10 = (bf16[192,3072]{1,0:T(8,128)(2,1)}, bf16[192,3072]{1,0:T(8,128)(2,1)}, u32[]{:S(2)}, u32[]{:S(2)}) collective-permute-start(bf16[192,3072]{1,0:T(8,128)(2,1)} %collective-permute-done.6.refs_4_.refs_6_.refs_5_), channel_id=1, source_target_pairs={{0,1},{1,0},{2,3},{3,2},{4,5},{5,4},{6,7},{7,6},{8,9},{9,8},{10,11... | collective-permute-start | bytes 3538952 | tf_op jit(solution)/shard_map/ppermute | solution.py:320
  57.0 88.4 %copy-start = (f32[240,1536]{1,0:T(8,128)}, f32[240,1536]{1,0:T(8,128)S(1)}, u32[]{:S(2)}) copy-start(f32[240,1536]{1,0:T(8,128)S(1)} %transformed.2.refs_10_.refs_12_.refs_11_) | copy-start | bytes 4423684
  57.0 2.1 copy-start.6
  57.0 2.1 copy-start.7
  59.1 1.1 copy-start.8
  60.2 13.1 %copy-start.11 = (bf16[4,1,256,1536]{3,2,1,0:T(8,128)(2,1)S(1)}, bf16[4,1,256,1536]{3,2,1,0:T(8,128)(2,1)}, u32[]{:S(2)}) copy-start(bf16[4,1,256,1536]{3,2,1,0:T(8,128)(2,1)} %param.12) | copy-start | bytes 9437188
  60.2 13.1 %copy-start.15 = (bf16[1536,768]{1,0:T(8,128)(2,1)S(1)}, bf16[1536,768]{1,0:T(8,128)(2,1)}, u32[]{:S(2)}) copy-start(bf16[1536,768]{1,0:T(8,128)(2,1)} %w_tgt.3) | copy-start | bytes 7077892
  61.0 12.4 %collective-permute-start.12 = (f32[8,128]{1,0:T(8,128)S(1)}, f32[8,128]{1,0:T(8,128)S(1)}, u32[]{:S(2)}, u32[]{:S(2)}) collective-permute-start(f32[8,128]{1,0:T(8,128)S(1)} %get-tuple-element.82), channel_id=1, source_target_pairs={{0,1},{2,3},{4,5},{6,7},{8,9},{10,11},{12,13},{14,15},{16,17},{18,... | collective-permute-start | bytes 12296 | tf_op jit(solution)/shard_map/ppermute | solution.py:459
  62.5 27.7 %collective-permute-start.11 = (bf16[256,1536]{1,0:T(8,128)(2,1)S(1)}, bf16[256,1536]{1,0:T(8,128)(2,1)S(1)}, u32[]{:S(2)}, u32[]{:S(2)}) collective-permute-start(bf16[256,1536]{1,0:T(8,128)(2,1)S(1)} %get-tuple-element.81), channel_id=1, source_target_pairs={{0,8},{2,10},{4,12},{6,14}} | collective-permute-start | bytes 2359304 | tf_op jit(solution)/shard_map/ppermute | solution.py:449
  73.4 4.7 %copy-start.9 = (bf16[256,1536]{1,0:T(8,128)(2,1)S(1)}, bf16[256,1536]{1,0:T(8,128)(2,1)}, u32[]{:S(2)}) copy-start(bf16[256,1536]{1,0:T(8,128)(2,1)} %get-tuple-element.68.refs_0_) | copy-start | bytes 2359300
  78.0 21.1 %copy-start.10 = (bf16[256,1536]{1,0:T(8,128)(2,1)S(1)}, bf16[256,1536]{1,0:T(8,128)(2,1)}, u32[]{:S(2)}) copy-start(bf16[256,1536]{1,0:T(8,128)(2,1)} %get-tuple-element.67.refs_0_) | copy-start | bytes 2359300
  88.7 24.7 %copy-start.17 = (s32[4,1,64,100]{3,2,1,0:T(8,128)S(1)}, s32[4,1,64,100]{3,2,1,0:T(8,128)}, u32[]{:S(2)}) copy-start(s32[4,1,64,100]{3,2,1,0:T(8,128)} %param.19) | copy-start | bytes 307204
  88.7 10.3 %collective-permute-start.13 = (bf16[256,1536]{1,0:T(8,128)(2,1)S(1)}, bf16[256,1536]{1,0:T(8,128)(2,1)S(1)}, u32[]{:S(2)}, u32[]{:S(2)}) collective-permute-start(bf16[256,1536]{1,0:T(8,128)(2,1)S(1)} %get-tuple-element.83), channel_id=1, source_target_pairs={{1,9},{3,11},{5,13},{7,15}} | collective-permute-start | bytes 2359304 | tf_op jit(solution)/shard_map/ppermute | solution.py:449
  109.3 14.5 %collective-permute-start.14 = (bf16[256,1536]{1,0:T(8,128)(2,1)S(1)}, bf16[256,1536]{1,0:T(8,128)(2,1)S(1)}, u32[]{:S(2)}, u32[]{:S(2)}) collective-permute-start(bf16[256,1536]{1,0:T(8,128)(2,1)S(1)} %get-tuple-element.84), channel_id=1, source_target_pairs={{0,8},{8,16},{1,9},{9,17},{2,10},{10,18},{3,11},{11,19},{4,12},{12... | collective-permute-start | bytes 2359304 | tf_op jit(solution)/shard_map/ppermute | solution.py:518
  113.5 10.3 %copy-start.13 = (bf16[256,1536]{1,0:T(8,128)(2,1)S(1)}, bf16[256,1536]{1,0:T(8,128)(2,1)}, u32[]{:S(2)}) copy-start(bf16[256,1536]{1,0:T(8,128)(2,1)} %get-tuple-element.66.refs_0_) | copy-start | bytes 2359300
  113.5 10.3 %collective-permute-start.15 = (s32[4,64,100]{2,1,0:T(8,128)S(1)}, s32[4,64,100]{2,1,0:T(8,128)S(1)}, u32[]{:S(2)}, u32[]{:S(2)}) collective-permute-start(s32[4,64,100]{2,1,0:T(8,128)S(1)} %bitcast.48), channel_id=1, source_target_pairs={{0,24},{1,25},{2,26},{3,27},{4,28},{5,29},{6,30},{7,31}} | collective-permute-start | bytes 307208 | tf_op jit(solution)/shard_map/ppermute | solution.py:480
  115.6 18.4 %copy-start.3 = (bf16[4,256,768]{2,1,0:T(8,128)(2,1)}, bf16[4,256,768]{2,1,0:T(8,128)(2,1)S(1)}, u32[]{:S(2)}) copy-start(bf16[4,256,768]{2,1,0:T(8,128)(2,1)S(1)} %targets.3.refs_16_.tgt_ref) | copy-start | bytes 4718596
  115.6 29.7 %copy-start.12 = (bf16[256,1536]{1,0:T(8,128)(2,1)S(1)}, bf16[256,1536]{1,0:T(8,128)(2,1)}, u32[]{:S(2)}) copy-start(bf16[256,1536]{1,0:T(8,128)(2,1)} %get-tuple-element.65.refs_0_) | copy-start | bytes 2359300
  134.1 11.3 %collective-permute-start.16 = (bf16[256,1536]{1,0:T(8,128)(2,1)S(1)}, bf16[256,1536]{1,0:T(8,128)(2,1)S(1)}, u32[]{:S(2)}, u32[]{:S(2)}) collective-permute-start(bf16[256,1536]{1,0:T(8,128)(2,1)S(1)} %get-tuple-element.88), channel_id=1, source_target_pairs={{0,8},{8,16},{16,24},{1,9},{9,17},{17,25},{2,10},{10,18},{18,26},{... | collective-permute-start | bytes 2359304 | tf_op jit(solution)/shard_map/ppermute | solution.py:518
  136.5 0.7 collective-permute-start.17
  156.3 13.6 %collective-permute-start.18 = (bf16[256,1536]{1,0:T(8,128)(2,1)}, bf16[256,1536]{1,0:T(8,128)(2,1)S(1)}, u32[]{:S(2)}, u32[]{:S(2)}) collective-permute-start(bf16[256,1536]{1,0:T(8,128)(2,1)} %get-tuple-element.92), channel_id=1, source_target_pairs={{0,8},{8,16},{16,24},{24,0},{1,9},{9,17},{17,25},{25,1},{2,10},{10... | collective-permute-start | bytes 2359304 | tf_op jit(solution)/shard_map/ppermute | solution.py:518
  158.3 2.5 collective-permute-start.19
  159.7 1.1 copy-start.1
  181.5 12.7 %collective-permute-start.20 = (bf16[256,1536]{1,0:T(8,128)(2,1)S(1)}, bf16[256,1536]{1,0:T(8,128)(2,1)S(1)}, u32[]{:S(2)}, u32[]{:S(2)}) collective-permute-start(bf16[256,1536]{1,0:T(8,128)(2,1)S(1)} %get-tuple-element.100), channel_id=1, source_target_pairs={{0,8},{8,16},{16,24},{24,0},{1,9},{9,17},{17,25},{25,1},{2,10},{10... | collective-permute-start | bytes 2359304 | tf_op jit(solution)/shard_map/ppermute | solution.py:518
  205.7 0.7 collective-permute-start.21
  206.5 46.2 %copy-start.2 = (f32[240,1536]{1,0:T(8,128)S(1)}, f32[240,1536]{1,0:T(8,128)}, u32[]{:S(2)}) copy-start(f32[240,1536]{1,0:T(8,128)} %copy-done.1) | copy-start | bytes 4423684
  206.5 7.4 %collective-permute-start.22 = (bf16[16,128]{1,0:T(8,128)(2,1)S(1)}, bf16[16,128]{1,0:T(8,128)(2,1)S(1)}, u32[]{:S(2)}, u32[]{:S(2)}) collective-permute-start(bf16[16,128]{1,0:T(8,128)(2,1)S(1)} %slice.78), channel_id=1, source_target_pairs={{0,1},{2,3},{4,5},{6,7},{8,9},{10,11},{12,13},{14,15},{16,17},{18,... | collective-permute-start | bytes 12296 | tf_op jit(solution)/shard_map/ppermute | solution.py:512
  213.9 14.5 %collective-permute-start.23 = (bf16[256,1536]{1,0:T(8,128)(2,1)S(1)}, bf16[256,1536]{1,0:T(8,128)(2,1)S(1)}, u32[]{:S(2)}, u32[]{:S(2)}) collective-permute-start(bf16[256,1536]{1,0:T(8,128)(2,1)S(1)} %get-tuple-element.102), channel_id=1, source_target_pairs={{1,9},{3,11},{5,13},{7,15},{9,17},{11,19},{13,21},{15,23},{17,25},... | collective-permute-start | bytes 2359304 | tf_op jit(solution)/shard_map/ppermute | solution.py:449
  240.0 12.7 %collective-permute-start.24 = (bf16[256,1536]{1,0:T(8,128)(2,1)S(1)}, bf16[256,1536]{1,0:T(8,128)(2,1)S(1)}, u32[]{:S(2)}, u32[]{:S(2)}) collective-permute-start(bf16[256,1536]{1,0:T(8,128)(2,1)S(1)} %get-tuple-element.104), channel_id=1, source_target_pairs={{0,8},{8,16},{16,24},{24,0},{1,9},{9,17},{17,25},{25,1},{2,10},{10... | collective-permute-start | bytes 2359304 | tf_op jit(solution)/shard_map/ppermute | solution.py:518
  263.1 10.2 %collective-permute-start.25 = (bf16[256,1536]{1,0:T(8,128)(2,1)S(1)}, bf16[256,1536]{1,0:T(8,128)(2,1)S(1)}, u32[]{:S(2)}, u32[]{:S(2)}) collective-permute-start(bf16[256,1536]{1,0:T(8,128)(2,1)S(1)} %get-tuple-element.105.x_ref), channel_id=1, source_target_pairs={{0,8},{8,16},{16,24},{1,9},{9,17},{17,25},{2,10},{10,18},{18,26},{... | collective-permute-start | bytes 2359304 | tf_op jit(solution)/shard_map/ppermute | solution.py:518
  274.9 0.7 collective-permute-start.26
  275.6 2.3 copy-start.5
  276.9 1.5 copy-start.4
  276.9 3.5 %collective-permute-start.27 = (bf16[256,1536]{1,0:T(8,128)(2,1)S(1)}, bf16[256,1536]{1,0:T(8,128)(2,1)S(1)}, u32[]{:S(2)}, u32[]{:S(2)}) collective-permute-start(bf16[256,1536]{1,0:T(8,128)(2,1)S(1)} %get-tuple-element.107.x_ref), channel_id=1, source_target_pairs={{16,24},{17,25},{18,26},{19,27},{20,28},{21,29},{22,30},{23,31}} | collective-permute-start | bytes 2359304 | tf_op jit(solution)/shard_map/ppermute | solution.py:518
  282.6 2.6 collective-permute-start.30
  283.2 55.4 %collective-permute-start.28 = (f32[4,64]{1,0:T(4,128)S(1)}, f32[4,64]{1,0:T(4,128)S(1)}, u32[]{:S(2)}, u32[]{:S(2)}) collective-permute-start(f32[4,64]{1,0:T(4,128)S(1)} %get-tuple-element.127), channel_id=1, source_target_pairs={{24,0},{25,1},{26,2},{27,3},{28,4},{29,5},{30,6},{31,7}} | collective-permute-start | bytes 3080 | tf_op jit(solution)/shard_map/ppermute | solution.py:528
  284.5 54.1 %collective-permute-start.29 = (f32[4,64]{1,0:T(4,128)S(1)}, f32[4,64]{1,0:T(4,128)S(1)}, u32[]{:S(2)}, u32[]{:S(2)}) collective-permute-start(f32[4,64]{1,0:T(4,128)S(1)} %get-tuple-element.125), channel_id=1, source_target_pairs={{24,8},{25,9},{26,10},{27,11},{28,12},{29,13},{30,14},{31,15}} | collective-permute-start | bytes 3080 | tf_op jit(solution)/shard_map/ppermute | solution.py:528
Sparse Core Ops, SparseCore 0:
  59.2 60.7 all-gather.1
